TPU v7x, 32 devices: a whole 2x2x4 slice. The times are simulated.
32 devices in a mesh: dp: 16 (over z, y, x), tensor: 2 (over core).
Axes of the slice: x: 2, y: 2, z: 4, core: 2. Of those that a mesh axis runs over, the one named last changes fastest.
Arguments:
- hidden_in: bfloat16 [64, 512, 1024], P('dp', 'tensor'), may hold values from -6 to 6
- segment_ids: int32 [64, 512], P('dp'), may hold values from 0 to 7, as said below
- adapter_pick: int32 [64], P('dp'), may hold values from 0 to 7
- w_qkv: bfloat16 [3, 1024, 1024], P(None, 'dp', 'tensor'), may hold values from -0.1875 to 0.1875
- w_out: bfloat16 [1024, 1024], P('tensor', 'dp'), may hold values from -0.5 to 0.5
- w_up: bfloat16 [1024, 4096], P('dp', 'tensor'), may hold values from -0.1875 to 0.1875
- w_down: bfloat16 [4096, 1024], P('tensor', 'dp'), may hold values from -0.09375 to 0.09375
- ln_gain: float32 [2, 1024], replicated, may hold values from 0.5 to 1.5
- ln_bias: float32 [2, 1024], replicated, may hold values from -1.5 to 1.5
- adapt_a: bfloat16 [4, 8, 1024, 16], replicated, may hold values from -0.1875 to 0.1875
- adapt_b: bfloat16 [4, 8, 16, 1024], replicated, may hold values from -0.75 to 0.75
- up_a: bfloat16 [8, 1024, 16], replicated, may hold values from -0.1875 to 0.1875
- up_b: bfloat16 [8, 16, 4096], replicated, may hold values from -0.75 to 0.75
- down_a: bfloat16 [8, 4096, 16], replicated, may hold values from -0.09375 to 0.09375
- down_b: bfloat16 [8, 16, 1024], replicated, may hold values from -0.75 to 0.75
- grad_out: bfloat16 [64, 512, 1024], P('dp', 'tensor'), may hold values from -6 to 6
Outputs:
- layer_out: bfloat16 [64, 512, 1024], P('dp', 'tensor')
- grad_in: float32 [64, 512, 1024], P('dp', 'tensor')
- grad_adapt_a: float32 [4, 8, 1024, 16], replicated
- grad_adapt_b: float32 [4, 8, 16, 1024], replicated
- grad_up_a: float32 [8, 1024, 16], replicated
- grad_up_b: float32 [8, 16, 4096], replicated
- grad_down_a: float32 [8, 4096, 16], replicated
- grad_down_b: float32 [8, 16, 1024], replicated
Inputs may be any that keep to these rules, and one draw needn't show every extreme that they name: `segment_ids`: within a sequence the ids start at 0 and rise by one at each new document, never falling; a sequence holds at most 8 documents. Among the sequences 4 k to 4 (k + 1) - 1, one holds a single document and another holds 8.
All inputs are finite; a program needn't handle non-finite values.
Results may differ from a plain program's by a relative error of at most 0.015.
Values may be sent and summed in bfloat16 or wider, within the bound.
No kernel may reach another device: no remote copies, remote signals or barrier semaphores. Data moves between devices by JAX's collectives and lax.ppermute only.
A program may use at most 256 MiB of HBM per device.

v0:
```python
import jax
import jax.numpy as jnp
from jax import lax
from jax.sharding import PartitionSpec as P

HEAD_DIM = 64


HIGHEST = lax.Precision.HIGHEST


def layer_norm_parts(values, gain_row, bias_row):
    centre = jnp.mean(values, axis=-1, keepdims=True)
    centred = values - centre
    variance = jnp.mean(centred * centred, axis=-1, keepdims=True)
    inverse = lax.rsqrt(variance + 1e-06)
    normed = centred * inverse
    return (normed * gain_row + bias_row, normed, inverse)


def layer_norm_back(gradient, normed, inverse, gain_row):
    scaled = gradient * gain_row
    mean_grad = jnp.mean(scaled, axis=-1, keepdims=True)
    mean_proj = jnp.mean(scaled * normed, axis=-1, keepdims=True)
    return (scaled - mean_grad - normed * mean_proj) * inverse


def select_rows(onehot, stacked):
    return jnp.einsum("se,e...->s...", onehot, stacked, preferred_element_type=jnp.float32).astype(
        jnp.bfloat16
    )


def fold_rows(onehot_wide, per_sequence):
    return jnp.einsum("se,s...->e...", onehot_wide, per_sequence, precision=HIGHEST)


def place_into(section, offset, length_all, along):
    new_shape = list(section.shape)
    new_shape[along] = length_all
    return lax.dynamic_update_slice_in_dim(
        jnp.zeros(new_shape, section.dtype), section, offset, along
    )


def project(inputs, weight, factor_one, factor_two):
    base_term = jnp.einsum("snd,df->snf", inputs, weight, preferred_element_type=jnp.float32)
    rank_part = jnp.einsum("snd,sdr->snr", inputs, factor_one, preferred_element_type=jnp.float32)
    low_rank = jnp.einsum(
        "snr,srf->snf", rank_part, factor_two.astype(jnp.float32), precision=HIGHEST
    )
    return (base_term + low_rank, rank_part)


def project_back(gradient, inputs, rank_part, weight, factor_one, factor_two):
    grad_rank = jnp.einsum("snf,srf->snr", gradient, factor_two, preferred_element_type=jnp.float32)
    grad_inputs = jnp.einsum("snf,df->snd", gradient, weight, preferred_element_type=jnp.float32)
    grad_inputs = grad_inputs + jnp.einsum(
        "snr,sdr->snd", grad_rank, factor_one.astype(jnp.float32), precision=HIGHEST
    )
    grad_first_factor = jnp.einsum(
        "snd,snr->sdr", inputs.astype(jnp.float32), grad_rank, precision=HIGHEST
    )
    grad_second_factor = jnp.einsum(
        "snr,snf->srf", rank_part, gradient.astype(jnp.float32), precision=HIGHEST
    )
    return (grad_inputs, grad_first_factor, grad_second_factor)


def masked_scores(queries, key_rows, query_segs, key_segs):
    scores = jnp.einsum(
        "qhe,khe->hqk", queries, key_rows, preferred_element_type=jnp.float32
    ) * HEAD_DIM ** (-0.5)
    same_doc = query_segs[:, None] == key_segs[None, :]
    return jnp.where(same_doc[None], scores, jnp.float32(-1000000000.0))


def attend(bundle):
    queries, key_rows, value_rows, query_segs, key_segs = bundle
    scores = masked_scores(queries, key_rows, query_segs, key_segs)
    row_peak = jnp.max(scores, axis=-1, keepdims=True)
    weights = jnp.exp(scores - row_peak)
    row_total = jnp.sum(weights, axis=-1, keepdims=True)
    probabilities = (weights / row_total).astype(jnp.bfloat16)
    mixture = jnp.einsum(
        "hqk,khe->qhe", probabilities, value_rows, preferred_element_type=jnp.float32
    )
    return (mixture.astype(jnp.bfloat16), (row_peak + jnp.log(row_total))[..., 0])


def attend_back(bundle):
    queries, key_rows, value_rows, query_segs, key_segs, log_total, grad_mixture = bundle
    scores = masked_scores(queries, key_rows, query_segs, key_segs)
    probabilities = jnp.exp(scores - log_total[..., None])
    grad_probs = jnp.einsum(
        "qhe,khe->hqk", grad_mixture, value_rows, preferred_element_type=jnp.float32
    )
    grad_values = jnp.einsum(
        "hqk,qhe->khe",
        probabilities.astype(jnp.bfloat16),
        grad_mixture,
        preferred_element_type=jnp.float32,
    )
    inner_sum = jnp.sum(grad_probs * probabilities, axis=-1, keepdims=True)
    grad_scores = (probabilities * (grad_probs - inner_sum)).astype(jnp.bfloat16)
    grad_queries = jnp.einsum(
        "hqk,khe->qhe", grad_scores, key_rows, preferred_element_type=jnp.float32
    ) * HEAD_DIM ** (-0.5)
    grad_keys = jnp.einsum(
        "hqk,qhe->khe", grad_scores, queries, preferred_element_type=jnp.float32
    ) * HEAD_DIM ** (-0.5)
    return (grad_queries.astype(jnp.bfloat16), grad_keys, grad_values)


def gelu_back(hidden_units, grad_act):
    _, pullback = jax.vjp(lambda pre_act: jax.nn.gelu(pre_act, approximate=False), hidden_units)
    return pullback(grad_act)[0]


def shards(
    hidden_in,
    segment_ids,
    adapter_pick,
    w_qkv,
    w_out,
    w_up,
    w_down,
    ln_gain,
    ln_bias,
    adapt_a,
    adapt_b,
    up_a,
    up_b,
    down_a,
    down_b,
    grad_out,
):
    qkv_full, out_full, up_rows, down_cols = (
        lax.all_gather(w_qkv, "dp", axis=1, tiled=True),
        lax.all_gather(w_out, "dp", axis=1, tiled=True),
        lax.all_gather(w_up, "dp", axis=0, tiled=True),
        lax.all_gather(w_down, "dp", axis=1, tiled=True),
    )
    sequences = hidden_in.shape[0]
    model_width = hidden_in.shape[2]
    ff_local = up_rows.shape[1]
    ff_all = up_b.shape[2]
    tensor_index = lax.axis_index("tensor")
    ff_offset = tensor_index * ff_local
    onehot_wide = (adapter_pick[:, None] == jnp.arange(adapt_a.shape[1])[None, :]).astype(
        jnp.float32
    )
    onehot = onehot_wide.astype(jnp.bfloat16)
    qkv_use, out_use = (qkv_full, out_full)
    qkv_in = lax.all_gather(hidden_in, "tensor", axis=1, tiled=True)
    width_use = qkv_full.shape[2]
    offset_use = tensor_index * width_use
    heads_use = width_use // HEAD_DIM
    rows_in = qkv_in.shape[1]
    factors_one, factors_two, rank_parts, heads_qkv = ([], [], [], [])
    for slot_index in range(3):
        factor_one = select_rows(onehot, adapt_a[slot_index])
        factor_two = select_rows(
            onehot, lax.dynamic_slice_in_dim(adapt_b[slot_index], offset_use, width_use, 2)
        )
        projected, rank_part = project(qkv_in, qkv_use[slot_index], factor_one, factor_two)
        factors_one.append(factor_one)
        factors_two.append(factor_two)
        rank_parts.append(rank_part)
        heads_qkv.append(
            projected.astype(jnp.bfloat16).reshape(sequences, rows_in, heads_use, HEAD_DIM)
        )
    key_all, value_all = (heads_qkv[1], heads_qkv[2])
    mixture, log_total = lax.map(
        attend, (heads_qkv[0], key_all, value_all, segment_ids, segment_ids)
    )
    attention = mixture.reshape(sequences, rows_in, width_use)
    out_one = select_rows(onehot, lax.dynamic_slice_in_dim(adapt_a[3], offset_use, width_use, 1))
    out_two = select_rows(onehot, adapt_b[3])
    branch_part, rank_out = project(attention, out_use, out_one, out_two)
    branch = lax.psum_scatter(branch_part, "tensor", scatter_dimension=1, tiled=True)
    middle, normed_one, inverse_one = layer_norm_parts(
        hidden_in.astype(jnp.float32) + branch, ln_gain[0], ln_bias[0]
    )
    middle_low = middle.astype(jnp.bfloat16)
    up_weight, down_weight = (up_rows, down_cols)
    mlp_inputs = lax.all_gather(middle_low, "tensor", axis=1, tiled=True)
    up_section = lax.dynamic_slice_in_dim(up_b, ff_offset, ff_local, 2)
    down_section = lax.dynamic_slice_in_dim(down_a, ff_offset, ff_local, 1)
    up_one = select_rows(onehot, up_a)
    up_two = select_rows(onehot, up_section)
    down_one = select_rows(onehot, down_section)
    down_two = select_rows(onehot, down_b)
    hidden_units, rank_up = project(mlp_inputs, up_weight, up_one, up_two)
    activation = jax.nn.gelu(hidden_units, approximate=False).astype(jnp.bfloat16)
    feed_part, rank_down = project(activation, down_weight, down_one, down_two)
    feed_sum = lax.psum_scatter(
        feed_part.astype(jnp.bfloat16), "tensor", scatter_dimension=1, tiled=True
    ).astype(jnp.float32)
    result, normed_two, inverse_two = layer_norm_parts(middle + feed_sum, ln_gain[1], ln_bias[1])
    layer_out = result.astype(jnp.bfloat16)
    grad_second = layer_norm_back(grad_out.astype(jnp.float32), normed_two, inverse_two, ln_gain[1])
    grad_feed = grad_second.astype(jnp.bfloat16)
    grad_feed_all = lax.all_gather(grad_feed, "tensor", axis=1, tiled=True)
    grad_act, grad_down_one, grad_down_two = project_back(
        grad_feed_all, activation, rank_down, down_weight, down_one, down_two
    )
    grad_hidden = gelu_back(hidden_units, grad_act).astype(jnp.bfloat16)
    grad_mlp_part, grad_up_one, grad_up_two = project_back(
        grad_hidden, mlp_inputs, rank_up, up_weight, up_one, up_two
    )
    folded_up_two = fold_rows(onehot_wide, grad_up_two)
    folded_down_one = fold_rows(onehot_wide, grad_down_one)
    grad_mlp = lax.psum_scatter(grad_mlp_part, "tensor", scatter_dimension=1, tiled=True)
    folded_up_two = place_into(folded_up_two, ff_offset, ff_all, 2)
    folded_down_one = place_into(folded_down_one, ff_offset, ff_all, 1)
    grad_first = layer_norm_back(grad_second + grad_mlp, normed_one, inverse_one, ln_gain[0])
    grad_branch = lax.all_gather(grad_first.astype(jnp.bfloat16), "tensor", axis=1, tiled=True)
    grad_attention, grad_out_one, grad_out_two = project_back(
        grad_branch, attention, rank_out, out_use, out_one, out_two
    )
    grad_mixture = grad_attention.astype(jnp.bfloat16).reshape(
        sequences, rows_in, heads_use, HEAD_DIM
    )
    grad_query, grad_key_wide, grad_value_wide = lax.map(
        attend_back,
        (heads_qkv[0], key_all, value_all, segment_ids, segment_ids, log_total, grad_mixture),
    )
    grad_key = grad_key_wide.astype(jnp.bfloat16)
    grad_value = grad_value_wide.astype(jnp.bfloat16)
    grad_input_part = jnp.zeros(qkv_in.shape, jnp.float32)
    folded_one, folded_two = ([], [])
    for slot_index, grad_heads in enumerate((grad_query, grad_key, grad_value)):
        flat_grad = grad_heads.reshape(sequences, rows_in, width_use)
        grad_inputs, grad_factor_one, grad_factor_two = project_back(
            flat_grad,
            qkv_in,
            rank_parts[slot_index],
            qkv_use[slot_index],
            factors_one[slot_index],
            factors_two[slot_index],
        )
        grad_input_part = grad_input_part + grad_inputs
        folded_one.append(fold_rows(onehot_wide, grad_factor_one))
        folded_two.append(
            place_into(fold_rows(onehot_wide, grad_factor_two), offset_use, model_width, 2)
        )
    folded_one.append(place_into(fold_rows(onehot_wide, grad_out_one), offset_use, model_width, 1))
    folded_two.append(fold_rows(onehot_wide, grad_out_two))
    grad_in = (
        lax.psum_scatter(
            grad_input_part.astype(jnp.bfloat16), "tensor", scatter_dimension=1, tiled=True
        ).astype(jnp.float32)
        + grad_first
    )
    totals = lax.psum(
        (
            jnp.stack(folded_one),
            jnp.stack(folded_two),
            fold_rows(onehot_wide, grad_up_one),
            folded_up_two,
            folded_down_one,
            fold_rows(onehot_wide, grad_down_two),
        ),
        ("dp", "tensor"),
    )
    return (layer_out, grad_in, totals[0], totals[1], totals[2], totals[3], totals[4], totals[5])


def solution(mesh):
    placed = (
        P("dp", "tensor", None),
        P("dp", None),
        P("dp"),
        P(None, "dp", "tensor"),
        P("tensor", "dp"),
        P("dp", "tensor"),
        P("tensor", "dp"),
        P(),
        P(),
        P(),
        P(),
        P(),
        P(),
        P(),
        P(),
        P("dp", "tensor", None),
    )
    return jax.shard_map(
        shards,
        mesh=mesh,
        in_specs=placed,
        out_specs=(P("dp", "tensor", None), P("dp", "tensor", None), P(), P(), P(), P(), P(), P()),
        check_vma=False,
    )
```

profile of v0, /device:TPU:0, one launch (start us, length us, event | category | flops | bytes accessed | tf_op | source)
XLA Modules:
  0.0 895.6 jit_solution(5443444405227223530)
XLA Ops:
  19.9 6.0 all-gather.9.cloned.1.call-done
  32.6 64.9 %all-gather.11.cloned.1.call-done = bf16[3,1024,512]{2,1,0:T(8,128)(2,1)} async-done(((bf16[3,64,512]{2,1,0:T(8,128)(2,1)}), bf16[3,1024,512]{2,1,0:T(8,128)(2,1)}) %all-gather.11.cloned.1.call-update) | async-done | bytes 3145744 | tf_op jit(solution)/shard_map/all_gather | solution.py:139
  107.5 15.8 %add_convert_fusion.5 = bf16[4,512,512]{1,2,0:T(8,128)(2,1)} fusion(f32[4,512,512]{1,2,0:T(8,128)S(1)} %fusion.87, f32[4,16,512]{2,1,0:T(8,128)S(1)} %copy-done.42, bf16[4,16,512]{2,0,1:T(4,128)(2,1)S(1)} %copy-done.49), kind=kOutput, calls=%fused_computation.110 | convolution fusion | flops 203423744 | bytes 6488064 | tf_op jit(solution)/shard_map/snr,srf->snf/dot_general | solution.py:49
  130.7 40.2 %while.26 = (s32[]{:T(128)}, bf16[4,512,8,64]{1,3,2,0:T(8,128)(2,1)}, f32[4,8,512]{2,1,0:T(8,128)}, bf16[4,512,8,64]{1,3,2,0:T(8,128)(2,1)}, s32[4,512]{1,0:T(4,...) while((s32[]{:T(128)}, bf16[4,512,8,64]{1,3,2,0:T(8,128)(2,1)}, ...), condition=%wide.region_3.4_spmd, body=%wide.region_0.3_spmd.sunk | while | flops 562556928 | bytes 28451416 | solution.py:174
  178.0 5.8 convolution_add_fusion.2
  185.7 14.2 %reduce-scatter.5.cloned.1.call-done = f32[4,256,1024]{2,1,0:T(8,128)} async-done(((f32[4,512,1024]{2,1,0:T(8,128)}), f32[4,256,1024]{2,1,0:T(8,128)}) %reduce-scatter.5.cloned.1.call-update) | async-done | bytes 4194320 | tf_op jit(solution)/shard_map/reduce_scatter | solution.py:181
  209.1 71.1 %all-gather.17.cloned.1.call-done = bf16[1024,2048]{1,0:T(8,128)(2,1)} async-done(((bf16[64,2048]{1,0:T(8,128)(2,1)}), bf16[1024,2048]{1,0:T(8,128)(2,1)}) %all-gather.17.cloned.1.call-update) | async-done | bytes 4194320 | tf_op jit(solution)/shard_map/all_gather | solution.py:141
  280.2 14.4 %all-gather.15.cloned.1.call-done = bf16[4,512,1024]{2,1,0:T(8,128)(2,1)} async-done(((bf16[4,256,1024]{2,1,0:T(8,128)(2,1)}), bf16[4,512,1024]{2,1,0:T(8,128)(2,1)}) %all-gather.15.cloned.1.call-update) | async-done | bytes 4194320 | tf_op jit(solution)/shard_map/all_gather | solution.py:187
  294.6 16.0 %fusion.67 = f32[4,512,2048]{2,1,0:T(8,128)} fusion(bf16[4,512,1024]{2,1,0:T(8,128)(2,1)} %all-gather.15.cloned.1.call-done, bf16[1024,2048]{1,0:T(8,128)(2,1)} %all-gather.17.cloned.1.call-done), kind=kOutput, calls=%fused_computation.94 | convolution fusion | flops 8589934592 | bytes 25165824 | tf_op jit(solution)/shard_map/snd,df->snf/dot_general | solution.py:47
  311.7 20.4 %fusion.71 = (u8[512,2048]{1,0:T(8,128)(4,1)S(1)}, u8[512,2048]{1,0:T(8,128)(4,1)S(1)}, f32[4,512,2048]{2,1,0:T(8,128)}) fusion(f32[4,512,2048]{2,1,0:T(8,128)} %fusion.67, f32[4,512,16]{1,2,0:T(8,128)S(1)} %fusion.130, bf16[4,16,2048]{2,0,1:T(4,128)(2,1)S(1)} %convolution_convert_fusion.1), kind=kOutput, calls=%fused_computation.115 | convolution fusion | flops 861929472 | bytes 36044800 | tf_op jit(solution)/shard_map/snr,srf->snf/dot_general | solution.py:49
  332.2 39.8 %multiply_convert_fusion.1 = (bf16[4,512,2048]{2,1,0:T(8,128)(2,1)S(1)}, f32[4,512,2048]{2,1,0:T(8,128)}) fusion(f32[4,512,2048]{2,1,0:T(8,128)} %get-tuple-element.191, u8[512,2048]{1,0:T(8,128)(4,1)S(1)} %get-tuple-element.122, u8[512,2048]{1,0:T(8,128)(4,1)S(1)} %get-tuple-element.121), kind=kLoop, calls=%fused_computation.72 | loop fusion | flops 293601280 | bytes 44040192 | tf_op jit(solution)/shard_map/convert_element_type | solution.py:195
  377.5 12.6 %fusion.63 = f32[4,512,1024]{2,1,0:T(8,128)S(1)} fusion(bf16[4,512,2048]{2,1,0:T(8,128)(2,1)} %copy-done.8, bf16[2048,1024]{0,1:T(8,128)(2,1)} %all-gather.19.cloned.1.call-done), kind=kOutput, calls=%fused_computation.90 | convolution fusion | flops 8589934592 | bytes 20971520 | tf_op jit(solution)/shard_map/snd,df->snf/dot_general | solution.py:47
  390.1 5.3 add_convert_fusion.2
  395.5 13.3 %reduce-scatter.7.cloned.1.call-done = bf16[4,256,1024]{2,1,0:T(8,128)(2,1)} async-done(((bf16[4,512,1024]{2,1,0:T(8,128)(2,1)}), bf16[4,256,1024]{2,1,0:T(8,128)(2,1)}) %reduce-scatter.7.cloned.1.call-update) | async-done | bytes 2097168 | tf_op jit(solution)/shard_map/reduce_scatter | solution.py:197
  419.8 15.1 %all-gather.21.cloned.1.call-done = bf16[4,512,1024]{2,1,0:T(8,128)(2,1)} async-done(((bf16[4,256,1024]{2,1,0:T(8,128)(2,1)}), bf16[4,512,1024]{2,1,0:T(8,128)(2,1)}) %all-gather.21.cloned.1.call-update) | async-done | bytes 4194320 | tf_op jit(solution)/shard_map/all_gather | solution.py:204
  434.9 15.7 %fusion.61 = f32[4,512,2048]{2,1,0:T(8,128)} fusion(bf16[4,512,1024]{2,1,0:T(8,128)(2,1)} %all-gather.21.cloned.1.call-done, bf16[2048,1024]{0,1:T(8,128)(2,1)} %all-gather.19.cloned.1.call-done), kind=kOutput, calls=%fused_computation.88 | convolution fusion | flops 8589934592 | bytes 25165824 | tf_op jit(solution)/shard_map/snf,df->snd/dot_general | solution.py:57
  451.8 20.5 %add_convert_fusion = bf16[4,512,2048]{2,1,0:T(8,128)(2,1)S(1)} fusion(f32[4,512,2048]{2,1,0:T(8,128)} %get-tuple-element.171, f32[4,512,2048]{2,1,0:T(8,128)} %fusion.61, f32[4,512,2048]{2,1,0:T(8,128)} %get-tuple-element.191, f32[4,512,16]{1,2,0:T(8,128)S(1)} %fusion.126, bf16[4,2048,16]{1,0,2:T(4,128)(2,1)S(1)} %convolution_convert_fusion), kind=kOutput, calls=%fused_computation.71 | convolution fusion | flops 868220928 | bytes 59113472 | tf_op jit(solution)/shard_map/snr,sdr->snd/dot_general | solution.py:58
  475.6 14.7 %fusion.65 = f32[4,512,1024]{2,1,0:T(8,128)S(1)} fusion(bf16[4,512,2048]{2,1,0:T(8,128)(2,1)S(1)} %add_convert_fusion, bf16[1024,2048]{1,0:T(8,128)(2,1)} %all-gather.17.cloned.1.call-done), kind=kOutput, calls=%fused_computation.92 | convolution fusion | flops 8589934592 | bytes 20971520 | tf_op jit(solution)/shard_map/snf,df->snd/dot_general | solution.py:57
  490.3 6.0 convolution_add_fusion.1
  496.4 18.1 %reduce-scatter.9.cloned.1.call-done = f32[4,256,1024]{2,1,0:T(8,128)} async-done(((f32[4,512,1024]{2,1,0:T(8,128)}), f32[4,256,1024]{2,1,0:T(8,128)}) %reduce-scatter.9.cloned.1.call-update) | async-done | bytes 4194320 | tf_op jit(solution)/shard_map/reduce_scatter | solution.py:214
  514.4 7.4 fusion.196
  534.8 7.0 fusion.214
  568.8 73.7 %while.27 = (s32[]{:T(128)}, bf16[4,512,8,64]{1,3,2,0:T(8,128)(2,1)}, bf16[4,512,8,64]{1,3,2,0:T(8,128)(2,1)}, bf16[4,512,8,64]{1,3,2,0:T(8,128)(2,1)}, bf16[4,5...) while((s32[]{:T(128)}, ...), condition=%wide.region_17.18_spmd, body=%wide.region_15.17_spmd.sunk | while | flops 1374679040 | bytes 95546568 | solution.py:225
  671.1 5.7 fusion.135
  676.8 5.6 fusion.139
  682.5 5.7 fusion.84
  688.2 5.7 fusion.86
  693.9 7.4 fusion.82
  701.3 18.5 %add_convert_fusion.1 = bf16[4,512,1024]{2,1,0:T(8,128)(2,1)} fusion(f32[4,512,1024]{2,1,0:T(8,128)} %fusion.82, f32[4,512,1024]{2,1,0:T(8,128)} %fusion.86, f32[4,512,1024]{2,1,0:T(8,128)} %fusion.135, f32[4,512,1024]{2,1,0:T(8,128)} %fusion.84, f32[4,512,1024]{2,1,0:T(8,128)} %fusion.139, f32[4,512,16]{1,2,0:T(8,128)S(1)} %fusion.155, ...), kind=kOutput, calls=%fused_computation.85 | convolution fusion | flops 415236096 | bytes 46399488 | tf_op jit(solution)/shard_map/snr,sdr->snd/dot_general | solution.py:58
  719.8 144.9 %all-reduce.3.cloned.1.call-done = (f32[4,8,1024,16]{2,1,3,0:T(8,128)}, f32[4,8,16,1024]{3,1,2,0:T(8,128)}, f32[8,1024,16]{1,0,2:T(8,128)}, f32[8,16,4096]{2,1,0...) async-done(((f32[4,8,1024,16]{2,1,3,0:T(8,128)}, f32[4,8,16,1024]{3,1,2,0:T(8,128)}, f32[8,1024,16]{1,0,2:T(8,128)}, f32[8,16,4096]{2,1,0:T(8,128)}, ...) | async-done | bytes 9437200 | tf_op jit(solution)/shard_map/psum | solution.py:256
  873.7 5.4 reduce-scatter.11.cloned.1.call-done
  879.1 6.1 convert_add_fusion
  (369 shorter events, 271.3 us)
Async XLA Ops:
  7.2 200.6 %copy-start = (bf16[8,16,4096]{2,1,0:T(8,128)(2,1)S(1)}, bf16[8,16,4096]{2,1,0:T(8,128)(2,1)}, u32[]{:S(2)}) copy-start(bf16[8,16,4096]{2,1,0:T(8,128)(2,1)} %param.32) | copy-start | bytes 3145732
  7.2 18.8 %all-gather.9.cloned.1.call-start = ((), (), s32[]{:S(2)}) async-start(), calls=%async_computation.4 | async-start | bytes 6291456 | tf_op jit(solution)/shard_map/all_gather | solution.py:155
  7.9 89.6 %all-gather.11.cloned.1.call-start = ((), (), s32[]{:S(2)}) async-start(), calls=%async_computation.5 | async-start | bytes 3342336 | tf_op jit(solution)/shard_map/all_gather | solution.py:139
  8.7 165.0 %all-gather.13.cloned.1.call-start = ((), (), s32[]{:S(2)}) async-start(), calls=%async_computation.6 | async-start | bytes 1114112 | tf_op jit(solution)/shard_map/all_gather | solution.py:140
  9.4 190.4 %reduce-scatter.5.cloned.1.call-start = ((), (), s32[]{:S(2)}) async-start(), calls=%async_computation.7 | async-start | bytes 12582912 | tf_op jit(solution)/shard_map/reduce_scatter | solution.py:181
  14.5 17.0 %copy-start.30 = (bf16[4,1024,16]{1,0,2:T(4,128)(2,1)}, bf16[4,1024,16]{1,0,2:T(4,128)(2,1)S(1)}, u32[]{:S(2)}) copy-start(bf16[4,1024,16]{1,0,2:T(4,128)(2,1)S(1)} %convolution_convert_fusion.6) | copy-start | bytes 393220
  15.6 15.8 %copy-start.34 = (bf16[4,1024,16]{1,0,2:T(4,128)(2,1)}, bf16[4,1024,16]{1,0,2:T(4,128)(2,1)S(1)}, u32[]{:S(2)}) copy-start(bf16[4,1024,16]{1,0,2:T(4,128)(2,1)S(1)} %convolution_convert_fusion.5) | copy-start | bytes 393220
  17.8 13.7 %copy-start.32 = (bf16[4,1024,16]{1,0,2:T(4,128)(2,1)}, bf16[4,1024,16]{1,0,2:T(4,128)(2,1)S(1)}, u32[]{:S(2)}) copy-start(bf16[4,1024,16]{1,0,2:T(4,128)(2,1)S(1)} %convolution_convert_fusion.7) | copy-start | bytes 393220
  19.9 158.0 %copy-start.36 = (bf16[4,16,1024]{2,0,1:T(4,128)(2,1)}, bf16[4,16,1024]{2,0,1:T(4,128)(2,1)S(1)}, u32[]{:S(2)}) copy-start(bf16[4,16,1024]{2,0,1:T(4,128)(2,1)S(1)} %convolution_convert_fusion.4) | copy-start | bytes 393220
  29.5 73.2 %copy-start.40 = (f32[4,16,512]{2,1,0:T(8,128)}, f32[4,16,512]{2,1,0:T(8,128)S(1)}, u32[]{:S(2)}) copy-start(f32[4,16,512]{2,1,0:T(8,128)S(1)} %fusion.141) | copy-start | bytes 393220
  32.6 93.1 %copy-start.38 = (f32[4,16,512]{2,1,0:T(8,128)}, f32[4,16,512]{2,1,0:T(8,128)S(1)}, u32[]{:S(2)}) copy-start(f32[4,16,512]{2,1,0:T(8,128)S(1)} %fusion.144) | copy-start | bytes 393220
  130.7 40.2 %copy-start.51 = (bf16[4,512,16]{1,0,2:T(4,128)(2,1)S(1)}, bf16[4,512,16]{1,0,2:T(4,128)(2,1)}, u32[]{:S(2)}) copy-start(bf16[4,512,16]{1,0,2:T(4,128)(2,1)} %convolution_convert_fusion.8) | copy-start | bytes 196612
  183.8 16.1 %copy-start.21 = (bf16[4,256,1024]{2,1,0:T(8,128)(2,1)S(1)}, bf16[4,256,1024]{2,1,0:T(8,128)(2,1)}, u32[]{:S(2)}) copy-start(bf16[4,256,1024]{2,1,0:T(8,128)(2,1)} %param.20) | copy-start | bytes 6291460
  183.8 96.4 %all-gather.17.cloned.1.call-start = ((), (), s32[]{:S(2)}) async-start(), calls=%async_computation.9 | async-start | bytes 4456448 | tf_op jit(solution)/shard_map/all_gather | solution.py:141
  184.4 110.2 %all-gather.15.cloned.1.call-start = ((), (), s32[]{:S(2)}) async-start(), calls=%async_computation.8 | async-start | bytes 6291456 | tf_op jit(solution)/shard_map/all_gather | solution.py:187
  185.7 17.5 %copy-start.70 = (f32[1,1024]{1,0:T(1,128)}, f32[1,1024]{1,0:T(1,128)S(1)}, u32[]{:S(2)}) copy-start(f32[1,1024]{1,0:T(1,128)S(1)} %get-tuple-element.190) | copy-start | bytes 12292
  202.5 319.4 %copy-start.61 = (f32[4,256]{1,0:T(4,128)}, f32[4,256]{1,0:T(4,128)S(1)}, u32[]{:S(2)}) copy-start(f32[4,256]{1,0:T(4,128)S(1)} %broadcast_multiply_fusion.5) | copy-start | bytes 12292
  203.1 318.8 %copy-start.63 = (f32[4,256]{1,0:T(4,128)}, f32[4,256]{1,0:T(4,128)S(1)}, u32[]{:S(2)}) copy-start(f32[4,256]{1,0:T(4,128)S(1)} %add_rsqrt_fusion.1) | copy-start | bytes 12292
  206.6 170.9 %all-gather.19.cloned.1.call-start = ((), (), s32[]{:S(2)}) async-start(), calls=%async_computation.10 | async-start | bytes 4456448 | tf_op jit(solution)/shard_map/all_gather | solution.py:142
  207.4 201.4 %reduce-scatter.7.cloned.1.call-start = ((), (), s32[]{:S(2)}) async-start(), calls=%async_computation.11 | async-start | bytes 6291456 | tf_op jit(solution)/shard_map/reduce_scatter | solution.py:197
  294.6 16.0 %copy-start.18 = (bf16[4,512,1024]{2,1,0:T(8,128)(2,1)S(1)}, bf16[4,512,1024]{2,1,0:T(8,128)(2,1)}, u32[]{:S(2)}) copy-start(bf16[4,512,1024]{2,1,0:T(8,128)(2,1)} %all-gather.15.cloned.1.call-done) | copy-start | bytes 12582916
  395.4 13.4 %copy-start.71 = (f32[1,1024]{1,0:T(1,128)S(1)}, f32[1,1024]{1,0:T(1,128)}, u32[]{:S(2)}) copy-start(f32[1,1024]{1,0:T(1,128)} %copy-done.70) | copy-start | bytes 12292
  395.4 39.5 %all-gather.21.cloned.1.call-start = ((), (), s32[]{:S(2)}) async-start(), calls=%async_computation.12 | async-start | bytes 6291456 | tf_op jit(solution)/shard_map/all_gather | solution.py:204
  419.8 94.7 %reduce-scatter.9.cloned.1.call-start = ((), (), s32[]{:S(2)}) async-start(), calls=%async_computation.13 | async-start | bytes 12582912 | tf_op jit(solution)/shard_map/reduce_scatter | solution.py:214
  434.9 15.7 %copy-start.15 = (bf16[4,512,1024]{2,1,0:T(8,128)(2,1)S(1)}, bf16[4,512,1024]{2,1,0:T(8,128)(2,1)}, u32[]{:S(2)}) copy-start(bf16[4,512,1024]{2,1,0:T(8,128)(2,1)} %all-gather.21.cloned.1.call-done) | copy-start | bytes 12582916
  496.3 18.1 %copy-start.72 = (f32[1,1024]{1,0:T(1,128)S(1)}, f32[1,1024]{1,0:T(1,128)}, u32[]{:S(2)}) copy-start(f32[1,1024]{1,0:T(1,128)} %get-tuple-element.189) | copy-start | bytes 12292
  496.3 57.3 %all-gather.23.cloned.1.call-start = ((), (), s32[]{:S(2)}) async-start(), calls=%async_computation.14 | async-start | bytes 6291456 | tf_op jit(solution)/shard_map/all_gather | solution.py:218
  526.1 338.6 %all-reduce.3.cloned.1.call-start = ((), (), s32[]{:S(2)}) async-start(), calls=%async_computation.16 | async-start | bytes 18874368 | tf_op jit(solution)/shard_map/psum | solution.py:256
  568.8 73.7 %copy-start.43 = (f32[4,16,512]{2,1,0:T(8,128)S(1)}, f32[4,16,512]{2,1,0:T(8,128)}, u32[]{:S(2)}) copy-start(f32[4,16,512]{2,1,0:T(8,128)} %fusion.137) | copy-start | bytes 393220
  568.8 77.2 %copy-start.50 = (bf16[4,16,512]{2,0,1:T(4,128)(2,1)S(1)}, bf16[4,16,512]{2,0,1:T(4,128)(2,1)}, u32[]{:S(2)}) copy-start(bf16[4,16,512]{2,0,1:T(4,128)(2,1)} %convolution_convert_fusion.9) | copy-start | bytes 196612
  670.2 208.9 %reduce-scatter.11.cloned.1.call-start = ((), (), s32[]{:S(2)}) async-start(), calls=%async_computation.15 | async-start | bytes 6291456 | tf_op jit(solution)/shard_map/reduce_scatter | solution.py:251
  873.7 11.6 %copy-start.26 = (f32[8,16,4096]{2,1,0:T(8,128)S(1)}, f32[8,16,4096]{2,1,0:T(8,128)}, u32[]{:S(2)}) copy-start(f32[8,16,4096]{2,1,0:T(8,128)} %get-tuple-element.368) | copy-start | bytes 6291460
  (70 other events, 344.0 us)
Sparse Core Ops, SparseCore 0:
  9.6 16.3 all-gather.8
  28.7 68.7 all-gather.10
  100.3 54.3 all-gather.12
  183.9 15.8 reduce-scatter.4
  202.8 77.3 all-gather.16
  282.2 12.2 all-gather.14
  297.7 77.2 all-gather.18
  395.5 13.1 reduce-scatter.6
  419.9 14.9 all-gather.20
  496.4 17.9 reduce-scatter.8
  526.2 14.9 all-gather.22
  670.4 194.2 all-reduce.2
  866.9 12.1 reduce-scatter.10
where the time goes:
time: 906 us; the launch traced here: 896 us
  waiting for transfers between devices  371 us (41%)
  matrix products  365 us (40%)
  other arithmetic  93.8 us (10%)
  local copies, waits for them, and re-layouts  49.8 us (5%)
  between operations  15 us (2%)
    psum x1, waiting for transfers between devices, shards(): lax.psum((jnp.stack(folded_one), jnp.stack(folded_two), fold_rows(onehot_...  145 us
    all_gather x1, waiting for transfers between devices, shards(): lax.all_gather(w_up, 'dp', axis=0, tiled=True)  71.1 us
    all_gather x1, waiting for transfers between devices, shards(): lax.all_gather(w_qkv, 'dp', axis=1, tiled=True)  64.9 us
    dot_general x6, matrix products, project_back(): jnp.einsum('snr,sdr->snd', grad_rank, factor_one.astype(jnp.float32), pre...  59.8 us
    dot_general x6, matrix products, project(): jnp.einsum('snr,srf->snf', rank_part, factor_two.astype(jnp.float32), pre...  52.7 us
    dot_general x6, matrix products, project_back(): jnp.einsum('snf,df->snd', gradient, weight, preferred_element_type=jnp.fl...  51.7 us
    dot_general x6, matrix products, project(): jnp.einsum('snd,df->snf', inputs, weight, preferred_element_type=jnp.floa...  43 us
    convert_element_type x1, other arithmetic, shards(): jax.nn.gelu(hidden_units, approximate=False).astype(jnp.bfloat16)  39.8 us
  transfers between devices with their start and end apart: 13, of which 10 were waited for; matrix products, arithmetic and copies ran while one was open for 30% of the time, Pallas kernels for 0%

commit v1 on v0

v1 whole, which is shorter than its diff:
```python
import functools

import jax
import jax.numpy as jnp
from jax import lax
from jax.experimental import pallas as pl
from jax.experimental.pallas import tpu as pltpu
from jax.sharding import PartitionSpec as P

HEAD_DIM = 64
BF = jnp.bfloat16
F32 = jnp.float32
LOG2E = 1.4426950408889634
VMEM = 60 * 2**20


def nn(a, b):
    return lax.dot_general(a, b, (((1,), (0,)), ((), ())), preferred_element_type=F32)


def nt(a, b):
    return lax.dot_general(a, b, (((1,), (1,)), ((), ())), preferred_element_type=F32)


def tn(a, b):
    return lax.dot_general(a, b, (((0,), (0,)), ((), ())), preferred_element_type=F32)


def params(flops, nbytes, limit=VMEM):
    return dict(
        compiler_params=pltpu.CompilerParams(vmem_limit_bytes=limit),
        cost_estimate=pl.CostEstimate(flops=flops, bytes_accessed=nbytes, transcendentals=0),
    )


def load_halves(gathered, scratch, sems, first, width):
    copies = []
    for half in range(2):
        copy = pltpu.make_async_copy(
            gathered.at[:, half, :, pl.ds(first, width)], scratch.at[half], sems.at[half]
        )
        copy.start()
        copies.append(copy)
    return copies


def rows_of(scratch, half, lo, width):
    block = scratch[half, :, :, pl.ds(lo, width)]
    return block.reshape(block.shape[0] * block.shape[1], width)


def qkv_kernel(meta, x_ref, a_ref, b_ref, w_ref, qkv_ref, rank_ref, w_scr, sems):
    @pl.when(pl.program_id(0) == 0)
    def _():
        for copy in load_halves(w_ref, w_scr, sems, 0, w_scr.shape[3]):
            copy.wait()

    x = x_ref[0]
    width = w_scr.shape[3] // 3
    for slot in range(3):
        rank = nt(x, a_ref[slot, 0]).astype(BF)
        rank_ref[0, slot] = rank
        for half in range(2):
            weight = rows_of(w_scr, half, slot * width, width)
            cols = slice(half * width, (half + 1) * width)
            full = nn(x, weight) + nn(rank, b_ref[slot, 0, :, cols])
            qkv_ref[0, slot, :, cols] = full.astype(BF)


def attend_kernel(q_ref, k_ref, v_ref, segc_ref, segr_ref, out_ref, lse_ref):
    q, k, v = q_ref[0, 0], k_ref[0, 0], v_ref[0, 0]
    length, lanes = q.shape
    lane = lax.broadcasted_iota(jnp.int32, (1, lanes), 1)
    zero = jnp.zeros((), BF)
    tile = 256
    stats = []
    for row in range(0, length, tile):
        same = segc_ref[0, row : row + tile, :] == segr_ref[0]
        total = jnp.zeros((tile, lanes), F32)
        for head in range(lanes // HEAD_DIM):
            mine = (lane // HEAD_DIM) == head
            scores = nt(q[row : row + tile], jnp.where(mine, k, zero)) * HEAD_DIM**-0.5
            scores = jnp.where(same, scores, F32(-1000000000.0))
            peak = jnp.max(scores, axis=1, keepdims=True)
            weights = jnp.exp(scores - peak)
            mass = jnp.sum(weights, axis=1, keepdims=True)
            probs = (weights * (1.0 / mass)).astype(BF)
            total += nn(probs, jnp.where(mine, v, zero))
            stats.append(peak + jnp.log(mass))
        out_ref[0, row : row + tile, :] = total.astype(BF)
    heads = lanes // HEAD_DIM
    spread = lax.broadcasted_iota(jnp.int32, (tile, 128), 1)
    for index in range(length // tile):
        table = jnp.zeros((tile, 128), F32)
        for head in range(heads):
            table = jnp.where(spread == head, stats[index * heads + head], table)
        lse_ref[0, 0, :, index * tile : (index + 1) * tile] = table.T[:8, :]


def attend_back_kernel(
    q_ref, k_ref, v_ref, segc_ref, segr_ref, lse_ref, o_ref, do_ref, gq_ref, gk_ref, gv_ref
):
    q, k, v, do = q_ref[0, 0], k_ref[0, 0], v_ref[0, 0], do_ref[0]
    length, lanes = q.shape
    lane = lax.broadcasted_iota(jnp.int32, (1, lanes), 1)
    zero = jnp.zeros((), BF)
    product = do.astype(F32) * o_ref[0].astype(F32)
    high = product.astype(BF)
    low = (product - high.astype(F32)).astype(BF)
    picker = (
        lax.broadcasted_iota(jnp.int32, (8, lanes), 0)
        == lax.broadcasted_iota(jnp.int32, (8, lanes), 1) // HEAD_DIM
    ).astype(BF)
    inner = nt(picker, high) + nt(picker, low)
    tile = 256
    scale = HEAD_DIM**-0.5
    grad_q = jnp.zeros((length, lanes), F32)
    for row in range(0, length, tile):
        same = segc_ref[0, row : row + tile, :] == segr_ref[0]
        grad_k = jnp.zeros((tile, lanes), F32)
        grad_v = jnp.zeros((tile, lanes), F32)
        for head in range(lanes // HEAD_DIM):
            mine = (lane // HEAD_DIM) == head
            k_mine = jnp.where(mine, k[row : row + tile], zero)
            v_mine = jnp.where(mine, v[row : row + tile], zero)
            scores = nt(k_mine, q) * scale
            scores = jnp.where(same, scores, F32(-1000000000.0))
            probs = jnp.exp(scores - lse_ref[0, 0, head : head + 1, :])
            grad_probs = nt(v_mine, do)
            grad_v += nn(probs.astype(BF), jnp.where(mine, do, zero))
            grad_scores = (probs * (grad_probs - inner[head : head + 1, :])).astype(BF)
            grad_k += nn(grad_scores, jnp.where(mine, q, zero))
            grad_q += tn(grad_scores, k_mine)
        gk_ref[0, 0, row : row + tile, :] = (grad_k * scale).astype(BF)
        gv_ref[0, 0, row : row + tile, :] = grad_v.astype(BF)
    gq_ref[0, 0] = (grad_q * scale).astype(BF)


def norm_parts(values):
    mean = jnp.mean(values, axis=-1, keepdims=True)
    centred = values - mean
    inverse = lax.rsqrt(jnp.mean(centred * centred, axis=-1, keepdims=True) + 1e-06)
    return centred * inverse, inverse


def norm_back(scaled, normed, inverse):
    mean_grad = jnp.mean(scaled, axis=-1, keepdims=True)
    mean_proj = jnp.mean(scaled * normed, axis=-1, keepdims=True)
    return (scaled - mean_grad - normed * mean_proj) * inverse


ROWS = 64


def out_kernel(
    meta, att_ref, x_ref, a_ref, b_ref, w_ref, gain_ref, bias_ref,
    normed_ref, inverse_ref, low_ref, rank_ref, w_scr, v_scr, sems,
):
    @pl.when(pl.program_id(0) == 0)
    def _():
        for copy in load_halves(w_ref, w_scr, sems, 3 * w_scr.shape[3], w_scr.shape[3]):
            copy.wait()

    att = att_ref[0]
    rank = nt(att, a_ref[0, 0]).astype(BF)
    rank_ref[0] = rank
    width = w_scr.shape[3]
    v_scr[...] = (
        nt(att[:, :width], rows_of(w_scr, 0, 0, width))
        + nt(att[:, width:], rows_of(w_scr, 1, 0, width))
        + nn(rank, b_ref[0, 0])
    )

    def step(index, carry):
        rows = pl.ds(pl.multiple_of(index * ROWS, ROWS), ROWS)
        normed, inverse = norm_parts(v_scr[rows, :] + x_ref[0, rows, :].astype(F32))
        normed_ref[0, rows, :] = normed
        inverse_ref[0, rows, :] = jnp.broadcast_to(inverse, (ROWS, 128))
        low_ref[0, rows, :] = (normed * gain_ref[0:1, :] + bias_ref[0:1, :]).astype(BF)
        return carry

    lax.fori_loop(0, v_scr.shape[0] // ROWS, step, 0)


def gelu_parts(x):
    density = jnp.exp(-0.5 * x * x)
    t = 1.0 / (1.0 + (0.3275911 * 0.7071067811865476) * jnp.abs(x))
    poly = t * (
        0.127414796
        + t * (-0.142248368 + t * (0.7107068705 + t * (-0.7265760135 + t * 0.5307027145)))
    )
    tail = poly * density
    phi = jnp.where(x > 0, 1.0 - tail, tail)
    return x * phi, phi + x * (density * 0.3989422804014327)


def up_kernel(
    meta, m_ref, a_ref, b_ref, w_ref, act_ref, slope_ref, rank_ref, w_scr, sems, *, first
):
    @pl.when(pl.program_id(0) == 0)
    def _():
        for copy in load_halves(w_ref, w_scr, sems, first, w_scr.shape[3]):
            copy.wait()

    m = m_ref[0]
    rank = nt(m, a_ref[0]).astype(BF)
    rank_ref[0] = rank
    width = w_scr.shape[3]
    chunk = 512
    per = width // chunk

    def step(index, carry):
        half = index // per
        lo = pl.multiple_of((index - half * per) * chunk, chunk)
        cols = pl.ds(pl.multiple_of(index * chunk, chunk), chunk)
        units = nn(m, rows_of(w_scr, half, lo, chunk)) + nn(rank, b_ref[0, :, cols])
        act, slope = gelu_parts(units)
        act_ref[0, :, cols] = act.astype(BF)
        slope_ref[0, :, cols] = slope.astype(BF)
        return carry

    lax.fori_loop(0, 2 * per, step, 0)


def down_kernel(
    meta, act_ref, slope_ref, n1_ref, go_ref, a_ref, b_ref, w_ref, gain_ref, bias_ref,
    out_ref, second_ref, gh_ref, ga_ref, gb_ref, w_scr, v_scr, gf_scr, sems, *, first,
):
    @pl.when(pl.program_id(0) == 0)
    def _():
        for copy in load_halves(w_ref, w_scr, sems, first, w_scr.shape[3]):
            copy.wait()

    act = act_ref[0]
    width = w_scr.shape[3]
    rank = nt(act, a_ref[0]).astype(BF)
    v_scr[...] = (
        nt(act[:, :width], rows_of(w_scr, 0, 0, width))
        + nt(act[:, width:], rows_of(w_scr, 1, 0, width))
        + nn(rank, b_ref[0])
    )

    def step(index, carry):
        rows = pl.ds(pl.multiple_of(index * ROWS, ROWS), ROWS)
        middle = n1_ref[0, rows, :] * gain_ref[0:1, :] + bias_ref[0:1, :]
        normed, inverse = norm_parts(v_scr[rows, :] + middle)
        out_ref[0, rows, :] = (normed * gain_ref[1:2, :] + bias_ref[1:2, :]).astype(BF)
        second = norm_back(go_ref[0, rows, :].astype(F32) * gain_ref[1:2, :], normed, inverse)
        second_ref[0, rows, :] = second
        gf_scr[rows, :] = second.astype(BF)
        return carry

    lax.fori_loop(0, v_scr.shape[0] // ROWS, step, 0)
    grad_feed = gf_scr[...]
    gb_ref[0] = tn(rank, grad_feed)
    grad_rank = nt(grad_feed, b_ref[0]).astype(BF)
    chunk = 512
    per = width // chunk

    def back(index, carry):
        half = index // per
        lo = pl.multiple_of((index - half * per) * chunk, chunk)
        cols = pl.ds(pl.multiple_of(index * chunk, chunk), chunk)
        grad_act = nn(grad_feed, rows_of(w_scr, half, lo, chunk)) + nn(grad_rank, a_ref[0, :, cols])
        gh_ref[0, :, cols] = (grad_act * slope_ref[0, :, cols].astype(F32)).astype(BF)
        ga_ref[0, :, cols] = tn(grad_rank, act_ref[0, :, cols])
        return carry

    lax.fori_loop(0, 2 * per, back, 0)


def mlp_back_kernel(
    meta, gh_ref, m_ref, n1_ref, r1_ref, second_ref, att_ref, ranku_ref, ranko_ref,
    ua_ref, ub_ref, oa_ref, ob_ref, w_ref, gain_ref,
    first_ref, gatt_ref, gua_ref, gub_ref, goa_ref, gob_ref,
    wu_scr, wo_scr, v_scr, gbr_scr, sems, semo, *, up_first, out_first,
):
    @pl.when(pl.program_id(0) == 0)
    def _():
        copies = load_halves(w_ref, wu_scr, sems, up_first, wu_scr.shape[3])
        copies += load_halves(w_ref, wo_scr, semo, out_first, wo_scr.shape[3])
        for copy in copies:
            copy.wait()

    gh = gh_ref[0]
    width = wu_scr.shape[3]
    grad_rank = nt(gh, ub_ref[0]).astype(BF)
    v_scr[...] = (
        nt(gh[:, :width], rows_of(wu_scr, 0, 0, width))
        + nt(gh[:, width:], rows_of(wu_scr, 1, 0, width))
        + nn(grad_rank, ua_ref[0])
    )
    gua_ref[0] = tn(grad_rank, m_ref[0])
    gub_ref[0] = tn(ranku_ref[0], gh)

    def step(index, carry):
        rows = pl.ds(pl.multiple_of(index * ROWS, ROWS), ROWS)
        scaled = (second_ref[0, rows, :] + v_scr[rows, :]) * gain_ref[0:1, :]
        first = norm_back(scaled, n1_ref[0, rows, :], r1_ref[0, rows, 0:1])
        first_ref[0, rows, :] = first
        gbr_scr[rows, :] = first.astype(BF)
        return carry

    lax.fori_loop(0, v_scr.shape[0] // ROWS, step, 0)
    grad_branch = gbr_scr[...]
    grad_rank_out = nt(grad_branch, ob_ref[0, 0]).astype(BF)
    goa_ref[0] = tn(grad_rank_out, att_ref[0])
    gob_ref[0] = tn(ranko_ref[0], grad_branch)
    owidth = wo_scr.shape[3]
    for half in range(2):
        cols = slice(half * owidth, (half + 1) * owidth)
        full = nn(grad_branch, rows_of(wo_scr, half, 0, owidth)) + nn(
            grad_rank_out, oa_ref[0, 0, :, cols]
        )
        gatt_ref[0, :, cols] = full.astype(BF)


def rank_back_kernel(meta, g_ref, x_ref, rank_ref, b_ref, gr_ref, ga_ref, gb_ref):
    grad = g_ref[0, 0]
    grad_rank = nt(b_ref[0, 0], grad).astype(BF)
    gr_ref[0, 0] = grad_rank
    ga_ref[0, 0] = nn(grad_rank, x_ref[0])
    gb_ref[0, 0] = tn(rank_ref[0, 0], grad)


def qkv_back_kernel(
    meta, gq_ref, gk_ref, gv_ref, gr_ref, first_ref, a_ref, w_ref, out_ref, w_scr, sems
):
    @pl.when(pl.program_id(0) == 0)
    def _():
        for copy in load_halves(w_ref, w_scr, sems, 0, w_scr.shape[3]):
            copy.wait()

    width = w_scr.shape[3] // 3
    total = first_ref[0]
    for slot, ref in enumerate((gq_ref, gk_ref, gv_ref)):
        total += tn(gr_ref[slot, 0], a_ref[slot, 0])
        for half in range(2):
            grad = ref[0, 0, :, half * width : (half + 1) * width]
            total += nt(grad, rows_of(w_scr, half, slot * width, width))
    out_ref[0] = total


def call(kernel, meta, grid, ins, outs, scratch, flops, **static):
    nbytes = sum(a.size * a.dtype.itemsize for a, _, _ in ins)
    in_specs = [
        pl.BlockSpec(memory_space=pl.ANY) if block is None else pl.BlockSpec(block, index)
        for _, block, index in ins
    ]
    return pl.pallas_call(
        functools.partial(kernel, **static) if static else kernel,
        grid_spec=pltpu.PrefetchScalarGridSpec(
            num_scalar_prefetch=1,
            grid=grid,
            in_specs=in_specs,
            out_specs=[pl.BlockSpec(block, index) for _, _, block, index in outs],
            scratch_shapes=scratch,
        ),
        out_shape=[jax.ShapeDtypeStruct(shape, dtype) for shape, dtype, _, _ in outs],
        **params(flops, nbytes),
    )(meta, *[a for a, _, _ in ins])


def shards(
    hidden_in, segment_ids, adapter_pick, w_qkv, w_out, w_up, w_down, ln_gain, ln_bias,
    adapt_a, adapt_b, up_a, up_b, down_a, down_b, grad_out,
):
    dp = lax.axis_size("dp")
    t = lax.axis_index("tensor")
    rows, ff_half = w_up.shape
    width = hidden_in.shape[2]
    half = width // 2
    ff = 2 * ff_half
    positions = hidden_in.shape[1]
    length = 2 * positions
    mine = hidden_in.shape[0] // 2
    rank = adapt_b.shape[2]
    adapters = adapt_b.shape[1]

    local = jnp.concatenate([w_qkv[0], w_qkv[1], w_qkv[2], w_out.T, w_up, w_down.T], axis=1)
    weights = lax.all_gather(local, ("dp", "tensor")).reshape(dp, 2, rows, local.shape[1])
    out_first = 3 * half
    up_first = 4 * half
    down_first = up_first + ff_half

    def to_sequences(pieces):
        other = lax.ppermute(
            [lax.dynamic_slice_in_dim(p, mine * (1 - t), mine, 0) for p in pieces], "tensor", [(0, 1), (1, 0)]
        )
        whole = []
        for piece, there in zip(pieces, other):
            here = lax.dynamic_slice_in_dim(piece, mine * t, mine, 0)
            low = jnp.where(t == 0, here, there)
            high = jnp.where(t == 0, there, here)
            whole.append(jnp.concatenate([low, high], axis=1))
        return whole

    def to_positions(value):
        here = lax.dynamic_slice_in_dim(value, positions * t, positions, 1)
        there = lax.ppermute(
            lax.dynamic_slice_in_dim(value, positions * (1 - t), positions, 1), "tensor", [(0, 1), (1, 0)]
        )
        low = jnp.where(t == 0, here, there)
        high = jnp.where(t == 0, there, here)
        return jnp.concatenate([low, high], axis=0)

    x, cotangent = to_sequences([hidden_in, grad_out])
    segs = lax.dynamic_slice_in_dim(segment_ids, mine * t, mine, 0)
    pick = lax.dynamic_slice_in_dim(adapter_pick, mine * t, mine, 0)
    meta = pick
    seg_col = segs.reshape(mine, length, 1)
    seg_row = segs.reshape(mine, 1, length)
    a_t = jnp.swapaxes(adapt_a, 2, 3)
    ua_t = jnp.swapaxes(up_a, 1, 2)
    da_t = jnp.swapaxes(down_a, 1, 2)

    blocks = dp
    tokens = mine * length
    seq3 = lambda s, m: (s, 0, 0)
    fixed2 = lambda s, m: (0, 0)
    picked3 = lambda s, m: (m[s], 0, 0)
    any_space = (None, None)

    def sems():
        return pltpu.SemaphoreType.DMA((2,))

    qkv, rank_qkv = call(
        qkv_kernel, meta, (mine,),
        [(x, (1, length, width), seq3),
         (a_t, (4, 1, rank, width), lambda s, m: (0, m[s], 0, 0)),
         (adapt_b, (4, 1, rank, width), lambda s, m: (0, m[s], 0, 0)),
         (weights, *any_space)],
        [((mine, 3, length, width), BF, (1, 3, length, width), lambda s, m: (s, 0, 0, 0)),
         ((mine, 3, length, rank), BF, (1, 3, length, rank), lambda s, m: (s, 0, 0, 0))],
        [pltpu.VMEM((2, blocks, rows, 3 * half), BF), sems()],
        6 * tokens * width * width,
    )

    pair = 2 * HEAD_DIM
    pairs = width // pair

    def slot_block(slot):
        return ((1, 1, length, pair), lambda s, h: (s, slot, 0, h))

    seg_specs = [
        pl.BlockSpec((1, length, 1), lambda s, h: (s, 0, 0)),
        pl.BlockSpec((1, 1, length), lambda s, h: (s, 0, 0)),
    ]
    attention, lse = pl.pallas_call(
        attend_kernel,
        grid=(mine, pairs),
        in_specs=[pl.BlockSpec(*slot_block(j)) for j in range(3)] + seg_specs,
        out_specs=[
            pl.BlockSpec((1, length, pair), lambda s, h: (s, 0, h)),
            pl.BlockSpec((1, 1, 8, length), lambda s, h: (s, h, 0, 0)),
        ],
        out_shape=[
            jax.ShapeDtypeStruct((mine, length, width), BF),
            jax.ShapeDtypeStruct((mine, pairs, 8, length), F32),
        ],
        **params(4 * tokens * length * width * 4, tokens * width * 8),
    )(qkv, qkv, qkv, seg_col, seg_row)

    normed, inverse, middle_low, rank_out = call(
        out_kernel, meta, (mine,),
        [(attention, (1, length, width), seq3),
         (x, (1, length, width), seq3),
         (a_t, (1, 1, rank, width), lambda s, m: (3, m[s], 0, 0)),
         (adapt_b, (1, 1, rank, width), lambda s, m: (3, m[s], 0, 0)),
         (weights, *any_space),
         (ln_gain, ln_gain.shape, fixed2),
         (ln_bias, ln_bias.shape, fixed2)],
        [((mine, length, width), F32, (1, length, width), seq3),
         ((mine, length, 128), F32, (1, length, 128), seq3),
         ((mine, length, width), BF, (1, length, width), seq3),
         ((mine, length, rank), BF, (1, length, rank), seq3)],
        [pltpu.VMEM((2, blocks, rows, half), BF), pltpu.VMEM((length, width), F32), sems()],
        2 * tokens * width * width,
    )

    act, slope, rank_up = call(
        up_kernel, meta, (mine,),
        [(middle_low, (1, length, width), seq3),
         (ua_t, (1, rank, width), picked3),
         (up_b, (1, rank, ff), picked3),
         (weights, *any_space)],
        [((mine, length, ff), BF, (1, length, ff), seq3),
         ((mine, length, ff), BF, (1, length, ff), seq3),
         ((mine, length, rank), BF, (1, length, rank), seq3)],
        [pltpu.VMEM((2, blocks, rows, ff_half), BF), sems()],
        2 * tokens * width * ff * 2,
        first=up_first,
    )

    layer_out, second, grad_hidden, g_down_a, g_down_b = call(
        down_kernel, meta, (mine,),
        [(act, (1, length, ff), seq3),
         (slope, (1, length, ff), seq3),
         (normed, (1, length, width), seq3),
         (cotangent, (1, length, width), seq3),
         (da_t, (1, rank, ff), picked3),
         (down_b, (1, rank, width), picked3),
         (weights, *any_space),
         (ln_gain, ln_gain.shape, fixed2),
         (ln_bias, ln_bias.shape, fixed2)],
        [((mine, length, width), BF, (1, length, width), seq3),
         ((mine, length, width), F32, (1, length, width), seq3),
         ((mine, length, ff), BF, (1, length, ff), seq3),
         ((mine, rank, ff), F32, (1, rank, ff), seq3),
         ((mine, rank, width), F32, (1, rank, width), seq3)],
        [pltpu.VMEM((2, blocks, rows, ff_half), BF), pltpu.VMEM((length, width), F32),
         pltpu.VMEM((length, width), BF), sems()],
        4 * tokens * width * ff,
        first=down_first,
    )

    grad_first, grad_att, g_up_a, g_up_b, g_out_a, g_out_b = call(
        mlp_back_kernel, meta, (mine,),
        [(grad_hidden, (1, length, ff), seq3),
         (middle_low, (1, length, width), seq3),
         (normed, (1, length, width), seq3),
         (inverse, (1, length, 128), seq3),
         (second, (1, length, width), seq3),
         (attention, (1, length, width), seq3),
         (rank_up, (1, length, rank), seq3),
         (rank_out, (1, length, rank), seq3),
         (ua_t, (1, rank, width), picked3),
         (up_b, (1, rank, ff), picked3),
         (a_t, (1, 1, rank, width), lambda s, m: (3, m[s], 0, 0)),
         (adapt_b, (1, 1, rank, width), lambda s, m: (3, m[s], 0, 0)),
         (weights, *any_space),
         (ln_gain, ln_gain.shape, fixed2)],
        [((mine, length, width), F32, (1, length, width), seq3),
         ((mine, length, width), BF, (1, length, width), seq3),
         ((mine, rank, width), F32, (1, rank, width), seq3),
         ((mine, rank, ff), F32, (1, rank, ff), seq3),
         ((mine, rank, width), F32, (1, rank, width), seq3),
         ((mine, rank, width), F32, (1, rank, width), seq3)],
        [pltpu.VMEM((2, blocks, rows, ff_half), BF), pltpu.VMEM((2, blocks, rows, half), BF),
         pltpu.VMEM((length, width), F32), pltpu.VMEM((length, width), BF), sems(), sems()],
        2 * tokens * width * (ff + width),
        up_first=up_first, out_first=out_first,
    )

    head_out = pl.BlockSpec((1, 1, length, pair), lambda s, h: (0, s, 0, h))
    grads_qkv = pl.pallas_call(
        attend_back_kernel,
        grid=(mine, pairs),
        in_specs=[pl.BlockSpec(*slot_block(j)) for j in range(3)]
        + seg_specs
        + [
            pl.BlockSpec((1, 1, 8, length), lambda s, h: (s, h, 0, 0)),
            pl.BlockSpec((1, length, pair), lambda s, h: (s, 0, h)),
            pl.BlockSpec((1, length, pair), lambda s, h: (s, 0, h)),
        ],
        out_specs=[head_out] * 3,
        out_shape=[jax.ShapeDtypeStruct((1, mine, length, width), BF)] * 3,
        **params(10 * tokens * length * width * 4, tokens * width * 16),
    )(qkv, qkv, qkv, seg_col, seg_row, lse, attention, grad_att)

    ranks, g_a, g_b = [], [], []
    for slot in range(3):
        by_seq = lambda s, m: (0, s, 0, 0)
        gr, ga, gb = call(
            rank_back_kernel, meta, (mine,),
            [(grads_qkv[slot], (1, 1, length, width), by_seq),
             (x, (1, length, width), seq3),
             (rank_qkv, (1, 1, length, rank), lambda s, m, slot=slot: (s, slot, 0, 0)),
             (adapt_b, (1, 1, rank, width), lambda s, m, slot=slot: (slot, m[s], 0, 0))],
            [((1, mine, rank, length), BF, (1, 1, rank, length), by_seq),
             ((1, mine, rank, width), F32, (1, 1, rank, width), by_seq),
             ((1, mine, rank, width), F32, (1, 1, rank, width), by_seq)],
            [],
            6 * tokens * width * rank,
        )
        ranks.append(gr)
        g_a.append(ga[0])
        g_b.append(gb[0])

    by_seq = lambda s, m: (0, s, 0, 0)
    grad_in = call(
        qkv_back_kernel, meta, (mine,),
        [(grads_qkv[0], (1, 1, length, width), by_seq),
         (grads_qkv[1], (1, 1, length, width), by_seq),
         (grads_qkv[2], (1, 1, length, width), by_seq),
         (jnp.concatenate(ranks, axis=0), (3, 1, rank, length), by_seq),
         (grad_first, (1, length, width), seq3),
         (a_t, (4, 1, rank, width), lambda s, m: (0, m[s], 0, 0)),
         (weights, *any_space)],
        [((mine, length, width), F32, (1, length, width), seq3)],
        [pltpu.VMEM((2, blocks, rows, 3 * half), BF), sems()],
        6 * tokens * width * width,
    )[0]

    onehot = (pick[:, None] == jnp.arange(adapters)[None, :]).astype(F32)

    def fold(per_sequence):
        total = onehot[0][:, None, None] * per_sequence[0][None]
        for index in range(1, mine):
            total += onehot[index][:, None, None] * per_sequence[index][None]
        return total.astype(BF)

    sums = lax.psum(
        tuple(fold(g) for g in [*g_a, g_out_a, *g_b, g_out_b, g_up_a, g_up_b, g_down_a, g_down_b]),
        ("dp", "tensor"),
    )
    sums = [s.astype(F32) for s in sums]
    turned = lambda v: jnp.swapaxes(v, -1, -2)
    return (
        to_positions(layer_out),
        to_positions(grad_in),
        turned(jnp.stack(sums[:4])),
        jnp.stack(sums[4:8]),
        turned(sums[8]),
        sums[9],
        turned(sums[10]),
        sums[11],
    )


def solution(mesh):
    placed = (
        P("dp", "tensor", None),
        P("dp", None),
        P("dp"),
        P(None, "dp", "tensor"),
        P("tensor", "dp"),
        P("dp", "tensor"),
        P("tensor", "dp"),
        P(),
        P(),
        P(),
        P(),
        P(),
        P(),
        P(),
        P(),
        P("dp", "tensor", None),
    )
    return jax.shard_map(
        shards,
        mesh=mesh,
        in_specs=placed,
        out_specs=(P("dp", "tensor", None), P("dp", "tensor", None), P(), P(), P(), P(), P(), P()),
        check_vma=False,
    )
```

time: 906 us -> 594 us (0.66); the launches traced: 896 us -> 593 us
  matrix products: 365 us -> 0 us
  Pallas kernels: 0 us -> 239 us
  waiting for transfers between devices: 371 us -> 286 us
  other arithmetic: 93.8 us -> 26.8 us
  local copies, waits for them, and re-layouts: 49.8 us -> 25.2 us
    dot_general x100 -> x0, matrix products: 365 us -> none  [the longest x6 59.8 us: project_back(): jnp.einsum('snr,sdr->snd', grad_rank, factor_one.astype(jnp.float32), pre...]
    pallas_call x0 -> x11, Pallas kernels: none -> 239 us  [the longest x9 178 us: call(): pl.pallas_call(functools.partial(kernel, **static) if static else kernel,...]
    convert_element_type x8 -> x4, other arithmetic: 57 us -> 5.43 us  [the longest x2 3.69 us: shards(): sums = [s.astype(F32) for s in sums]]
    reduce_scatter x4 -> x0, waiting for transfers between devices: 51 us -> none  [the longest x1 18.1 us: shards(): lax.psum_scatter(grad_mlp_part, 'tensor', scatter_dimension=1, tiled=True)]
    all_gather x8 -> x1, waiting for transfers between devices: 171 us -> 146 us  [shards(): lax.all_gather(local, ('dp', 'tensor')).reshape(dp, 2, rows, local.shape[1])]
    reduce_sum x10 -> x0, other arithmetic: 23.5 us -> none  [the longest x2 8.85 us: layer_norm_back(): mean_grad = jnp.mean(scaled, axis=-1, keepdims=True)]
    unnamed x160 -> x57, local copies, waits for them, and re-layouts: 24.1 us -> 8.54 us
  transfers between devices with their start and end apart: 13 -> 6, of which waited for: 10 -> 4; matrix products, arithmetic and copies ran while one was open for 30% -> 4% of each run, Pallas kernels for 0% -> 0%
where the time goes in v1:
time: 594 us; the launch traced here: 593 us
  waiting for transfers between devices  286 us (48%)
  Pallas kernels  239 us (40%)
  other arithmetic  26.8 us (5%)
  local copies, waits for them, and re-layouts  25.2 us (4%)
  between operations  14.4 us (2%)
    pallas_call x9, Pallas kernels, call(): pl.pallas_call(functools.partial(kernel, **static) if static else kernel,...  178 us
    all_gather x1, waiting for transfers between devices, shards(): lax.all_gather(local, ('dp', 'tensor')).reshape(dp, 2, rows, local.shape[1])  146 us
    psum x1, waiting for transfers between devices, shards(): lax.psum(tuple((fold(g) for g in [*g_a, g_out_a, *g_b, g_out_b, g_up_a, g...  136 us
    pallas_call x1, Pallas kernels, shards(): pl.pallas_call(attend_back_kernel, grid=(mine, pairs), in_specs=[pl.Block...  33.7 us
    pallas_call x1, Pallas kernels, shards(): pl.pallas_call(attend_kernel, grid=(mine, pairs), in_specs=[pl.BlockSpec(...  27.2 us
  transfers between devices with their start and end apart: 6, of which 4 were waited for; matrix products, arithmetic and copies ran while one was open for 4% of the time, Pallas kernels for 0%

profile of v1, /device:TPU:0, one launch (start us, length us, event | category | flops | bytes accessed | tf_op | source)
XLA Modules:
  0.0 592.9 jit_solution(7414770447046841722)
XLA Ops:
  13.7 2.3 constant_dynamic-slice_fusion.4
  19.3 1.2 collective-permute-done.1
  20.5 1.9 broadcast_select_fusion.3
  22.5 1.5 pad_maximum_fusion.1.x_ref
  24.0 1.5 pad_maximum_fusion.2.go_ref
  25.5 145.6 %all-gather.3.cloned.1.call-done = bf16[2048,6144]{1,0:T(8,128)(2,1)} async-done(((bf16[64,6144]{1,0:T(8,128)(2,1)}), bf16[2048,6144]{1,0:T(8,128)(2,1)}) %all-gather.3.cloned.1.call-update) | async-done | bytes 25165840 | tf_op jit(solution)/shard_map/all_gather | solution.py:381
  171.1 17.7 %shard_map.215 = (bf16[2,3,512,1024]{3,2,1,0:T(8,128)(2,1)}, bf16[2,3,512,16]{3,2,1,0:T(8,128)(2,1)}) custom-call(s32[2]{0:T(128)} %copy-done.24, bf16[2,512,1024]{2,1,0:T(8,128)(2,1)} %pad_maximum_fusion.1.x_ref, bf16[4,8,16,1024]{3,2,1,0:T(8,128)(2,1)} %bitcast.96, bf16[4,8,16,1024]{3,2,1,0:T(8,128)(2,1)} %b_ref.13, bf16[16,2,64,6144]{3,2,1,0:T(8,128)(2,1)} %bitcast.90), custom_call_target="tpu_custom_call" | custom-call | flops 6442450944 | bytes 29360128 | tf_op jit(solution)/shard_map/pallas_call | solution.py:350
  188.8 27.2 %shard_map.216 = (bf16[2,512,1024]{2,1,0:T(8,128)(2,1)}, f32[2,8,8,512]{3,2,1,0:T(8,128)}) custom-call(bf16[2,3,512,1024]{3,2,1,0:T(8,128)(2,1)} %get-tuple-element.42.q_ref.k_ref.v_ref, bf16[2,3,512,1024]{3,2,1,0:T(8,128)(2,1)} %get-tuple-element.42.q_ref.k_ref.v_ref, bf16[2,3,512,1024]{3,2,1,0:T(8,128)(2,1)} %get-tuple-element.42.q_ref.k_ref.v_ref, ...), custom_call_target="tpu_custom_call" | custom-call | flops 8589934592 | bytes 8388608 | tf_op jit(solution)/shard_map/pallas_call | solution.py:449
  215.9 13.3 %shard_map.217 = (f32[2,512,1024]{2,1,0:T(8,128)}, f32[2,512,128]{2,1,0:T(8,128)}, bf16[2,512,1024]{2,1,0:T(8,128)(2,1)}, bf16[2,512,16]{2,1,0:T(8,128)(2,1)}) custom-call(s32[2]{0:T(128)} %copy-done.24, bf16[2,512,1024]{2,1,0:T(8,128)(2,1)} %get-tuple-element.43.att_ref.o_ref, bf16[2,512,1024]{2,1,0:T(8,128)(2,1)} %pad_maximum_fusion.1.x_ref, ...), custom_call_target="tpu_custom_call" | custom-call | flops 2147483648 | bytes 31473664 | tf_op jit(solution)/shard_map/pallas_call | solution.py:350
  229.2 34.8 %shard_map.218 = (bf16[2,512,4096]{2,1,0:T(8,128)(2,1)}, bf16[2,512,4096]{2,1,0:T(8,128)(2,1)}, bf16[2,512,16]{2,1,0:T(8,128)(2,1)}) custom-call(s32[2]{0:T(128)} %copy-done.24, bf16[2,512,1024]{2,1,0:T(8,128)(2,1)} %get-tuple-element.44.m_ref, bf16[8,16,1024]{2,1,0:T(8,128)(2,1)} %bitcast.100, bf16[8,16,4096]{2,1,0:T(8,128)(2,1)} %ub_ref.1, ...), custom_call_target="tpu_custom_call" | custom-call | flops 17179869184 | bytes 28573696 | tf_op jit(solution)/shard_map/pallas_call | solution.py:350
  264.0 47.8 %shard_map.219 = (bf16[2,512,1024]{2,1,0:T(8,128)(2,1)}, f32[2,512,1024]{2,1,0:T(8,128)}, bf16[2,512,4096]{2,1,0:T(8,128)(2,1)}, f32[2,16,4096]{2,1,0:T(8,128)}, f32[2,16,1024]{2,1,0:T(8,128)}) custom-call(s32[2]{0:T(128)} %copy-done.24, bf16[2,512,4096]{2,1,0:T(8,128)(2,1)} %get-tuple-element.45.act_ref, bf16[2,512,4096]{2,1,0:T(8,128)(2,1)} %get-tuple-element.46.slope_ref, ...), custom_call_target="tpu_custom_call" | custom-call | flops 17179869184 | bytes 49561600 | tf_op jit(solution)/shard_map/pallas_call | solution.py:350
  311.8 34.6 %shard_map.220 = (f32[2,512,1024]{2,1,0:T(8,128)}, bf16[2,512,1024]{2,1,0:T(8,128)(2,1)}, f32[2,16,1024]{2,1,0:T(8,128)}, f32[2,16,4096]{2,1,0:T(8,128)}, f32[2,...) custom-call(s32[2]{0:T(128)} %copy-done.24, bf16[2,512,4096]{2,1,0:T(8,128)(2,1)} %get-tuple-element.50.gh_ref, ...), custom_call_target="tpu_custom_call" | custom-call | flops 10737418240 | bytes 50143232 | tf_op jit(solution)/shard_map/pallas_call | solution.py:350
  347.6 33.7 %shard_map.221 = (bf16[1,2,512,1024]{3,2,1,0:T(8,128)(2,1)}, bf16[1,2,512,1024]{3,2,1,0:T(8,128)(2,1)}, bf16[1,2,512,1024]{3,2,1,0:T(8,128)(2,1)}) custom-call(bf16[2,3,512,1024]{3,2,1,0:T(8,128)(2,1)} %get-tuple-element.42.q_ref.k_ref.v_ref, bf16[2,3,512,1024]{3,2,1,0:T(8,128)(2,1)} %get-tuple-element.42.q_ref.k_ref.v_ref, ...), custom_call_target="tpu_custom_call" | custom-call | flops 21474836480 | bytes 16777216 | tf_op jit(solution)/shard_map/pallas_call | solution.py:546
  381.3 4.5 shard_map.222
  387.5 4.3 shard_map.223
  393.7 4.5 shard_map.224
  400.0 1.4 pad_maximum_fusion.4.gr_ref
  401.4 17.0 %shard_map.225 = f32[2,512,1024]{2,1,0:T(8,128)} custom-call(s32[2]{0:T(128)} %copy-done.24, bf16[1,2,512,1024]{3,2,1,0:T(8,128)(2,1)} %get-tuple-element.56.g_ref.gq_ref, bf16[1,2,512,1024]{3,2,1,0:T(8,128)(2,1)} %get-tuple-element.57.g_ref.gk_ref, bf16[1,2,512,1024]{3,2,1,0:T(8,128)(2,1)} %get-tuple-element.58.g_ref.gv_ref, ...), custom_call_target="tpu_custom_call" | custom-call | flops 6442450944 | bytes 36798464 | tf_op jit(solution)/shard_map/pallas_call | solution.py:350
  418.4 3.2 constant_dynamic-slice_fusion
  421.7 1.9 fusion
  424.6 1.7 add_convert_fusion.2
  426.3 1.6 copy-done.4
  429.3 3.1 collective-permute-done.2
  433.0 1.5 pad_maximum_fusion.3
  434.5 1.5 copy-done.2
  436.0 2.1 dynamic-slice_select_fusion.1
  438.1 2.5 pad_maximum_fusion
  440.7 136.2 %all-reduce.3.cloned.1.call-done = (bf16[1,8,16,1024]{3,2,1,0:T(8,128)(2,1)}, bf16[1,8,16,1024]{3,2,1,0:T(8,128)(2,1)}, bf16[1,8,16,1024]{3,2,1,0:T(8,128)(2,1)}...) async-done(((bf16[1,8,16,1024]{3,2,1,0:T(8,128)(2,1)}, ...) | async-done | bytes 4718608 | tf_op jit(solution)/shard_map/psum | solution.py:603
  576.9 2.8 convert_element_type.66
  579.7 1.5 transpose.71
  583.0 1.5 maximum_convert_fusion
  584.5 1.5 convert_bitcast_fusion
  (91 shorter events, 21.1 us)
Async XLA Ops:
  7.2 10.4 %copy-start = (s32[4,512]{1,0:T(4,128)S(1)}, s32[4,512]{1,0:T(4,128)}, u32[]{:S(2)}) copy-start(s32[4,512]{1,0:T(4,128)} %param.17) | copy-start | bytes 24580
  7.2 163.9 %all-gather.3.cloned.1.call-start = ((), (), s32[]{:S(2)}) async-start(), calls=%async_computation | async-start | bytes 25952256 | tf_op jit(solution)/shard_map/all_gather | solution.py:381
  8.9 7.5 %copy-start.3 = (bf16[4,256,1024]{2,1,0:T(8,128)(2,1)S(1)}, bf16[4,256,1024]{2,1,0:T(8,128)(2,1)}, u32[]{:S(2)}) copy-start(bf16[4,256,1024]{2,1,0:T(8,128)(2,1)} %param.31) | copy-start | bytes 6291460
  12.7 0.9 copy-start.6
  13.6 563.2 %all-reduce.3.cloned.1.call-start = ((), (), s32[]{:S(2)}) async-start(), calls=%async_computation.1 | async-start | bytes 9437184 | tf_op jit(solution)/shard_map/psum | solution.py:603
  13.7 3.8 copy-start.25
  15.9 3.3 collective-permute-start
  17.4 3.1 collective-permute-start.1
  17.6 4.9 copy-start.24
  311.8 35.7 %copy-start.7 = (f32[2,16,4096]{2,1,0:T(8,128)S(1)}, f32[2,16,4096]{2,1,0:T(8,128)}, u32[]{:S(2)}) copy-start(f32[2,16,4096]{2,1,0:T(8,128)} %get-tuple-element.74) | copy-start | bytes 1572868
  381.2 5.4 copy-start.21
  393.7 6.3 %copy-start.20 = (f32[2,16,1024]{2,1,0:T(8,128)S(1)}, f32[2,16,1024]{2,1,0:T(8,128)}, u32[]{:S(2)}) copy-start(f32[2,16,1024]{2,1,0:T(8,128)} %get-tuple-element.71) | copy-start | bytes 393220
  393.7 6.3 %copy-start.19 = (f32[2,16,1024]{2,1,0:T(8,128)S(1)}, f32[2,16,1024]{2,1,0:T(8,128)}, u32[]{:S(2)}) copy-start(f32[2,16,1024]{2,1,0:T(8,128)} %get-tuple-element.67) | copy-start | bytes 393220
  393.7 6.3 %copy-start.22 = (bf16[1,2,16,512]{3,2,1,0:T(8,128)(2,1)S(1)}, bf16[1,2,16,512]{3,2,1,0:T(8,128)(2,1)}, u32[]{:S(2)}) copy-start(bf16[1,2,16,512]{3,2,1,0:T(8,128)(2,1)} %get-tuple-element.60) | copy-start | bytes 98308
  393.7 6.3 %copy-start.23 = (bf16[1,2,16,512]{3,2,1,0:T(8,128)(2,1)S(1)}, bf16[1,2,16,512]{3,2,1,0:T(8,128)(2,1)}, u32[]{:S(2)}) copy-start(bf16[1,2,16,512]{3,2,1,0:T(8,128)(2,1)} %get-tuple-element.61) | copy-start | bytes 98308
  421.6 3.0 copy-start.18
  421.6 12.9 %collective-permute-start.3 = (f32[2,256,1024]{2,1,0:T(8,128)}, f32[2,256,1024]{2,1,0:T(8,128)}, u32[]{:S(2)}, u32[]{:S(2)}) collective-permute-start(f32[2,256,1024]{2,1,0:T(8,128)} %constant_dynamic-slice_fusion), channel_id=1, source_target_pairs={{0,1},{1,0},{2,3},{3,2},{4,5},{5,4},{6,7},{7,6},{8,9},{9,8},{10,11... | collective-permute-start | bytes 6291464 | tf_op jit(solution)/shard_map/ppermute | solution.py:400
  426.3 1.6 copy-start.4
  428.9 3.5 collective-permute-start.2
  433.0 3.0 copy-start.2
  576.9 2.9 copy-start.5
  579.7 1.6 copy-start.17
  579.7 2.4 copy-start.16
  579.7 3.3 copy-start.12
  579.7 3.3 copy-start.13
  579.7 3.3 copy-start.14
  579.7 3.3 copy-start.15
  582.1 2.4 copy-start.8
  582.1 2.4 copy-start.9
  582.1 2.4 copy-start.10
  582.1 2.4 copy-start.11
  583.0 3.0 copy-start.1
Sparse Core Ops, SparseCore 0:
  13.7 157.3 all-gather.2
  426.4 150.3 all-reduce.2

commit v2 on v0

v2 whole, which is shorter than its diff:
```python
import functools

import jax
import jax.numpy as jnp
from jax import lax
from jax.experimental import pallas as pl
from jax.experimental.pallas import tpu as pltpu
from jax.sharding import PartitionSpec as P

HEAD_DIM = 64
BF = jnp.bfloat16
F32 = jnp.float32
LOG2E = 1.4426950408889634
VMEM = 60 * 2**20


def nn(a, b):
    return lax.dot_general(a, b, (((1,), (0,)), ((), ())), preferred_element_type=F32)


def nt(a, b):
    return lax.dot_general(a, b, (((1,), (1,)), ((), ())), preferred_element_type=F32)


def tn(a, b):
    return lax.dot_general(a, b, (((0,), (0,)), ((), ())), preferred_element_type=F32)


def params(flops, nbytes, limit=VMEM):
    return dict(
        compiler_params=pltpu.CompilerParams(vmem_limit_bytes=limit),
        cost_estimate=pl.CostEstimate(flops=flops, bytes_accessed=nbytes, transcendentals=0),
    )


class Piece:
    def __init__(self, col, width, rel, row, count, array, at, other):
        self.col, self.width, self.rel, self.row = col, width, rel, row
        self.count, self.array, self.at, self.other = count, array, at, other


class Loader:
    def __init__(self, plan, refs, scratch, sems, me, t):
        self.plan, self.refs, self.scratch, self.sems, self.me, self.t = plan, refs, scratch, sems, me, t

    def start(self):
        for slot, at, count, col, width, other, rel, row, into in self.plan:
            half = self.t ^ other
            if rel is None:
                source = self.refs[slot].at[:, half, :, pl.ds(col, width)]
                target = self.scratch.at[half]
            else:
                source = self.refs[slot].at[pl.ds(at, count), pl.ds(col, width)]
                target = self.scratch.at[half, self.me ^ rel, pl.ds(row, count), pl.ds(into, width)]
            pltpu.make_async_copy(source, target, self.sems.at[other]).start()

    def wait(self, other):
        whole = self.scratch.at[self.t ^ other]
        pltpu.make_async_copy(whole, whole, self.sems.at[other]).wait()

    def first_step(self):
        pl.when(pl.program_id(0) == 0)(self.start)

    def first_wait(self, other):
        pl.when(pl.program_id(0) == 0)(lambda: self.wait(other))

    def first_wait_all(self, index):
        if index == 0:
            self.first_wait(0)
            self.first_wait(1)

    def cols(self, half, lo, width):
        block = self.scratch[half, :, :, pl.ds(lo, width)]
        return block.reshape(block.shape[0] * block.shape[1], width)


def weight_plan(pieces, first, width):
    arrays, plan = [], []
    for p in pieces:
        lo, hi = max(p.col, first), min(p.col + p.width, first + width)
        if lo >= hi:
            continue
        slot = next((i for i, a in enumerate(arrays) if a is p.array), None)
        if slot is None:
            slot = len(arrays)
            arrays.append(p.array)
        plan.append((slot, p.at, p.count, lo - p.col, hi - lo, p.other, p.rel, p.row, lo - first))
    return arrays, plan


def qkv_kernel(meta, ins, outs, weights, scratch):
    x_ref, a_ref, b_ref = ins
    qkv_ref, rank_ref = outs
    (w,) = weights
    w.first_step()
    x = x_ref[0]
    slots, rank_size = rank_ref.shape[2] // a_ref.shape[2], a_ref.shape[2]
    rank = nt(x, a_ref[0:slots, 0].reshape(slots * rank_size, x.shape[1])).astype(BF)
    rank_ref[0] = rank
    width = w.scratch.shape[3] // slots
    for other in range(2):
        w.first_wait(other)
        half = w.t ^ other
        cols = pl.ds(pl.multiple_of(half * width, width), width)
        for slot in range(slots):
            mine = rank[:, slot * rank_size : (slot + 1) * rank_size]
            full = nn(x, w.cols(half, slot * width, width)) + nn(mine, b_ref[slot, 0, :, cols])
            qkv_ref[0, slot, :, cols] = full.astype(BF)


SCALE = HEAD_DIM**-0.5
SCALE2 = SCALE * LOG2E
GROUP = 4 * HEAD_DIM


def one_head(lane, head, value):
    return jnp.where(lane // HEAD_DIM == head, value, jnp.zeros((), value.dtype))


def attend_kernel(q_ref, k_ref, v_ref, segc_ref, segr_ref, out_ref, lse_ref):
    q, k, v = q_ref[0, 0], k_ref[0, 0], v_ref[0, 0]
    length, lanes = q.shape
    heads = lanes // HEAD_DIM
    lane = lax.broadcasted_iota(jnp.int32, (1, lanes), 1)
    same = segc_ref[0] == segr_ref[0]
    v_t = v.T

    def score(head):
        return nt(one_head(lane, head, k), q)

    mixed = []
    scores = score(0)
    for head in range(heads):
        following = score(head + 1) if head + 1 < heads else None
        masked = jnp.where(same, scores, F32(-1000000000.0 / SCALE))
        peak = jnp.max(masked, axis=0, keepdims=True) * SCALE2
        weights = jnp.exp2(masked * SCALE2 - peak)
        mass = jnp.sum(weights, axis=0, keepdims=True)
        rows = slice(head * HEAD_DIM, (head + 1) * HEAD_DIM)
        mixed.append(nn(v_t[rows, :], weights.astype(BF)) * (1.0 / mass))
        lse_ref[0, 0, head : head + 1, :] = peak + jnp.log2(mass)
        scores = following
    out_ref[0] = jnp.concatenate(mixed, axis=0).astype(BF).T
    lse_ref[0, 0, heads:, :] = jnp.zeros((lse_ref.shape[2] - heads, length), F32)


def attend_back_kernel(
    q_ref, k_ref, v_ref, segc_ref, segr_ref, lse_ref, o_ref, do_ref, gq_ref, gk_ref, gv_ref
):
    q, k, v, do = q_ref[0, 0], k_ref[0, 0], v_ref[0, 0], do_ref[0]
    lanes = q.shape[1]
    lane = lax.broadcasted_iota(jnp.int32, (1, lanes), 1)
    product = do.astype(F32) * o_ref[0].astype(F32)
    high = product.astype(BF)
    low = (product - high.astype(F32)).astype(BF)
    picker = (
        lax.broadcasted_iota(jnp.int32, (8, lanes), 0)
        == lax.broadcasted_iota(jnp.int32, (8, lanes), 1) // HEAD_DIM
    ).astype(BF)
    inner = nt(picker, high) + nt(picker, low)
    same = segc_ref[0] == segr_ref[0]
    grad_q = grad_k = grad_v = None
    for head in range(lanes // HEAD_DIM):
        k_mine = one_head(lane, head, k)
        masked = jnp.where(same, nt(k_mine, q), F32(-1000000000.0 / SCALE))
        probs = jnp.exp2(masked * SCALE2 - lse_ref[0, 0, head : head + 1, :])
        grad_probs = nt(one_head(lane, head, v), do)
        grad_scores = (probs * (grad_probs - inner[head : head + 1, :])).astype(BF)
        part_v = nn(probs.astype(BF), one_head(lane, head, do))
        part_k = nn(grad_scores, one_head(lane, head, q))
        part_q = tn(grad_scores, k_mine)
        grad_v = part_v if head == 0 else grad_v + part_v
        grad_k = part_k if head == 0 else grad_k + part_k
        grad_q = part_q if head == 0 else grad_q + part_q
    gq_ref[0] = (grad_q * SCALE).astype(BF)
    gk_ref[0] = (grad_k * SCALE).astype(BF)
    gv_ref[0] = grad_v.astype(BF)


def norm_parts(values):
    mean = jnp.mean(values, axis=-1, keepdims=True)
    centred = values - mean
    inverse = lax.rsqrt(jnp.mean(centred * centred, axis=-1, keepdims=True) + 1e-06)
    return centred * inverse, inverse


def norm_back(scaled, normed, inverse):
    mean_grad = jnp.mean(scaled, axis=-1, keepdims=True)
    mean_proj = jnp.mean(scaled * normed, axis=-1, keepdims=True)
    return (scaled - mean_grad - normed * mean_proj) * inverse


ROWS = 32


def by_rows(count, step):
    for row in range(0, count, ROWS):
        step(slice(row, row + ROWS))


def out_kernel(meta, ins, outs, weights, scratch):
    att_ref, x_ref, a_ref, b_ref, gain_ref, bias_ref = ins
    normed_ref, inverse_ref, low_ref, rank_ref = outs
    (w,) = weights
    (v_scr,) = scratch
    w.first_step()
    att = att_ref[0]
    rank = nt(att, a_ref[0, 0]).astype(BF)
    rank_ref[0] = rank
    width = w.scratch.shape[3]
    w.first_wait(0)
    w.first_wait(1)
    v_scr[...] = (
        nt(att[:, :width], w.cols(0, 0, width))
        + nt(att[:, width:], w.cols(1, 0, width))
        + nn(rank, b_ref[0, 0])
    )

    def step(rows):
        normed, inverse = norm_parts(v_scr[rows, :] + x_ref[0, rows, :].astype(F32))
        normed_ref[0, rows, :] = normed
        inverse_ref[0, rows, :] = jnp.broadcast_to(inverse, (ROWS, 128))
        low_ref[0, rows, :] = (normed * gain_ref[0:1, :] + bias_ref[0:1, :]).astype(BF)

    by_rows(v_scr.shape[0], step)


def gelu_parts(x):
    density = jnp.exp2((-0.5 * LOG2E) * x * x)
    t = 1.0 / (1.0 + (0.3275911 * 0.7071067811865476) * jnp.abs(x))
    poly = t * (
        0.127414796
        + t * (-0.142248368 + t * (0.7107068705 + t * (-0.7265760135 + t * 0.5307027145)))
    )
    tail = poly * density
    phi = jnp.where(x > 0, 1.0 - tail, tail)
    return x * phi, phi + x * (density * 0.3989422804014327)


CHUNK = 512


def up_kernel(meta, ins, outs, weights, scratch):
    m_ref, a_ref = ins[:2]
    b_refs = ins[2:]
    act_ref, slope_ref, rank_ref = outs
    (w,) = weights
    w.first_step()
    m = m_ref[0]
    rank = nt(m, a_ref[0]).astype(BF)
    rank_ref[0] = rank
    width = w.scratch.shape[3]
    for half, b_ref in enumerate(b_refs):
        w.first_wait_all(half)
        for lo in range(0, width, CHUNK):
            cols = slice(half * width + lo, half * width + lo + CHUNK)
            units = nn(m, w.cols(half, lo, CHUNK)) + nn(rank, b_ref[0, :, lo : lo + CHUNK])
            act, slope = gelu_parts(units)
            act_ref[0, :, cols] = act.astype(BF)
            slope_ref[0, :, cols] = slope.astype(BF)


def down_kernel(meta, ins, outs, weights, scratch):
    n1_ref, go_ref, a_ref, b_ref, gain_ref, bias_ref = ins[:6]
    parts = (len(ins) - 6) // 2
    act_refs, slope_refs = ins[6 : 6 + parts], ins[6 + parts :]
    out_ref, second_ref, gh_ref, ga_ref, gb_ref = outs
    (w,) = weights
    v_scr, gf_scr = scratch
    w.first_step()
    size = act_refs[0].shape[2] // 2
    places = [(half, p) for half in range(2) for p in range(parts)]
    start = lambda half, p: (half * parts + p) * size
    rank = sum(
        nt(act_refs[p][0, :, half * size : (half + 1) * size], a_ref[0, :, start(half, p) : start(half, p) + size])
        for half, p in places
    ).astype(BF)
    w.first_wait(0)
    w.first_wait(1)
    v_scr[...] = nn(rank, b_ref[0]) + sum(
        nt(act_refs[p][0, :, half * size : (half + 1) * size], w.cols(half, p * size, size))
        for half, p in places
    )

    def step(rows):
        middle = n1_ref[0, rows, :] * gain_ref[0:1, :] + bias_ref[0:1, :]
        normed, inverse = norm_parts(v_scr[rows, :] + middle)
        out_ref[0, rows, :] = (normed * gain_ref[1:2, :] + bias_ref[1:2, :]).astype(BF)
        second = norm_back(go_ref[0, rows, :].astype(F32) * gain_ref[1:2, :], normed, inverse)
        second_ref[0, rows, :] = second
        gf_scr[rows, :] = second.astype(BF)

    by_rows(v_scr.shape[0], step)
    grad_feed = gf_scr[...]
    gb_ref[0] = tn(rank, grad_feed).astype(BF)
    grad_rank = nt(grad_feed, b_ref[0]).astype(BF)
    for half, p in places:
        local = slice(half * size, (half + 1) * size)
        cols = slice(start(half, p), start(half, p) + size)
        grad_act = nn(grad_feed, w.cols(half, p * size, size)) + nn(grad_rank, a_ref[0, :, cols])
        gh_ref[0, :, cols] = (grad_act * slope_refs[p][0, :, local].astype(F32)).astype(BF)
        ga_ref[0, :, cols] = tn(grad_rank, act_refs[p][0, :, local]).astype(BF)


def mlp_back_kernel(meta, ins, outs, weights, scratch):
    (gh_ref, m_ref, n1_ref, r1_ref, second_ref, att_ref, ranku_ref, ranko_ref,
     ua_ref, ub_ref, oa_ref, ob_ref, gain_ref) = ins
    first_ref, gatt_ref, gua_ref, gub_ref, goa_ref, gob_ref = outs
    up, out = weights
    v_scr, gbr_scr = scratch
    up.first_step()
    out.first_step()
    width = up.scratch.shape[3]
    grad_rank = nt(gh_ref[0], ub_ref[0]).astype(BF)
    for loader in (up, out):
        loader.first_wait(0)
        loader.first_wait(1)
    v_scr[...] = (
        nt(gh_ref[0, :, :width], up.cols(0, 0, width))
        + nt(gh_ref[0, :, width:], up.cols(1, 0, width))
        + nn(grad_rank, ua_ref[0])
    )
    gua_ref[0] = tn(grad_rank, m_ref[0]).astype(BF)
    gub_ref[0] = tn(ranku_ref[0], gh_ref[0]).astype(BF)

    def step(rows):
        scaled = (second_ref[0, rows, :] + v_scr[rows, :]) * gain_ref[0:1, :]
        first = norm_back(scaled, n1_ref[0, rows, :], r1_ref[0, rows, 0:1])
        first_ref[0, rows, :] = first
        gbr_scr[rows, :] = first.astype(BF)

    by_rows(v_scr.shape[0], step)
    grad_branch = gbr_scr[...]
    grad_rank_out = nt(grad_branch, ob_ref[0, 0]).astype(BF)
    goa_ref[0] = tn(grad_rank_out, att_ref[0]).astype(BF)
    gob_ref[0] = tn(ranko_ref[0], grad_branch).astype(BF)
    owidth = out.scratch.shape[3]
    for half in range(2):
        cols = slice(half * owidth, (half + 1) * owidth)
        full = nn(grad_branch, out.cols(half, 0, owidth)) + nn(grad_rank_out, oa_ref[0, 0, :, cols])
        gatt_ref[0, :, cols] = full.astype(BF)


def rank_back_kernel(meta, ins, outs, weights, scratch):
    gq_ref, gk_ref, gv_ref, x_ref, rank_ref, b_ref = ins
    gr_ref, a_refs, b_refs = outs[0], outs[1:4], outs[4:]
    size = b_ref.shape[2]
    ranks = []
    for slot, ref in enumerate((gq_ref, gk_ref, gv_ref)):
        grad = ref[0]
        ranks.append(nt(b_ref[slot, 0], grad))
        b_refs[slot][0] = tn(rank_ref[0, :, slot * size : (slot + 1) * size], grad).astype(BF)
    stacked = jnp.concatenate(ranks, axis=0).astype(BF)
    gr_ref[0] = stacked
    products = nn(stacked, x_ref[0]).astype(BF)
    for slot, ref in enumerate(a_refs):
        ref[0] = products[slot * size : (slot + 1) * size]


def qkv_back_kernel(meta, ins, outs, weights, scratch):
    gq_ref, gk_ref, gv_ref, gr_ref, first_ref, a_ref = ins
    (out_ref,) = outs
    (w,) = weights
    w.first_step()
    slots = 3
    width = w.scratch.shape[3] // slots
    size = a_ref.shape[2]
    total = first_ref[0] + tn(
        gr_ref[0], a_ref[0:slots, 0].reshape(slots * size, out_ref.shape[2])
    )
    for other in range(2):
        w.first_wait(other)
        half = w.t ^ other
        cols = pl.ds(pl.multiple_of(half * width, width), width)
        for slot, ref in enumerate((gq_ref, gk_ref, gv_ref)):
            total += nt(ref[0, :, cols], w.cols(half, slot * width, width))
    out_ref[0] = total


def call(kernel, meta, ins, outs, flops, scratch=(), weights=(), limit=VMEM, after=()):
    plans = [weight_plan(pieces, first, width) for pieces, first, width, _, _ in weights]
    n_in, n_out, n_w = len(ins), len(outs), len(weights)
    counts = [len(arrays) for arrays, _ in plans]
    steps = meta.shape[0] - 2
    after = [a for a in after if a is not None]
    n_after = len(after)

    def body(meta_ref, *refs):
        refs = list(refs)
        take = lambda n: [refs.pop(0) for _ in range(n)]
        in_refs = take(n_in)
        w_refs = [take(n) for n in counts]
        take(n_after)
        out_refs = take(n_out)
        w_scr = take(n_w)
        w_sem = take(n_w)
        me, t = meta_ref[steps], meta_ref[steps + 1]
        loaders = [
            Loader(plan, r, s, m, me, t)
            for (_, plan), r, s, m in zip(plans, w_refs, w_scr, w_sem)
        ]
        kernel(meta_ref, in_refs, out_refs, loaders, refs)

    w_arrays = [a for arrays, _ in plans for a in arrays]
    nbytes = sum(a.size * a.dtype.itemsize for a, _, _ in ins)
    nbytes += sum(2 * dp * rows * width * 2 for _, _, width, dp, rows in weights)
    for shape, dtype, _, _ in outs:
        size = jnp.dtype(dtype).itemsize
        for extent in shape:
            size *= extent
        nbytes += size
    return pl.pallas_call(
        body,
        grid_spec=pltpu.PrefetchScalarGridSpec(
            num_scalar_prefetch=1,
            grid=(steps,),
            in_specs=[pl.BlockSpec(block, index) for _, block, index in ins]
            + [pl.BlockSpec(memory_space=pltpu.HBM) for _ in [*w_arrays, *after]],
            out_specs=[pl.BlockSpec(block, index) for _, _, block, index in outs],
            scratch_shapes=[pltpu.VMEM((2, dp, rows, width), BF) for _, _, width, dp, rows in weights]
            + [pltpu.SemaphoreType.DMA((2,)) for _ in weights]
            + list(scratch),
        ),
        out_shape=[pltpu.HBM(shape, dtype) for shape, dtype, _, _ in outs],
        **params(flops, nbytes, limit),
    )(meta, *[in_hbm(a) for a in [*[a for a, _, _ in ins], *w_arrays, *after]])


def pack(outs, fresh=(), after=()):
    after = [a for a in after if a is not None]
    arrays, plan, heights, widths = [], [], [], []

    def slot(array):
        for index, known in enumerate(arrays):
            if known is array:
                return index
        arrays.append(array)
        return len(arrays) - 1

    for index, parts in enumerate(outs):
        row = 0
        for part in parts:
            array, at, count, col, cols, into, advance = part
            plan.append((slot(array), at, count, col, cols, index, row, into))
            if advance:
                row += count
        heights.append(row)
        widths.append(max(part[4] + part[5] for part in parts))
    for array in after:
        slot(array)
    n_in = len(arrays)

    near = [any(a is f for f in fresh) for a in arrays]

    def kernel(*refs):
        ins, results, sems = refs[:n_in], refs[n_in:-1], refs[-1]
        copies = []
        for number, (a, at, count, col, cols, o, row, into) in enumerate(plan):
            source = ins[a].at[pl.ds(at, count), pl.ds(col, cols)]
            target = results[o].at[pl.ds(row, count), pl.ds(into, cols)]
            if not near[a]:
                copy = pltpu.make_async_copy(source, target, sems.at[number])
                copy.start()
                copies.append(copy)
        for a, at, count, col, cols, o, row, into in plan:
            if near[a]:
                results[o][pl.ds(row, count), pl.ds(into, cols)] = ins[a][pl.ds(at, count), pl.ds(col, cols)]
        for copy in copies:
            copy.wait()

    spaces = [pltpu.VMEM if n else pltpu.HBM for n in near]
    return pl.pallas_call(
        kernel,
        in_specs=[pl.BlockSpec(memory_space=space) for space in spaces],
        out_specs=[pl.BlockSpec(memory_space=pltpu.VMEM)] * len(outs),
        out_shape=[pltpu.VMEM(shape, BF) for shape in zip(heights, widths)],
        scratch_shapes=[pltpu.SemaphoreType.DMA((len(plan),))],
        compiler_params=pltpu.CompilerParams(vmem_limit_bytes=8 * 2**20),
        cost_estimate=pl.CostEstimate(
            flops=0, bytes_accessed=sum(h * w * 4 for h, w in zip(heights, widths)), transcendentals=0
        ),
    )(*[pltpu.with_memory_space_constraint(a, space) for a, space in zip(arrays, spaces)])


def in_hbm(array):
    return pltpu.with_memory_space_constraint(array, pltpu.HBM)


X, Y, Z1, Z2, Z3 = 1, 2, 4, 8, 12
ZS = (Z1, Z2, Z3)


def hop(array, bits):
    return lax.ppermute(array, "dp", [(i, i ^ bits) for i in range(lax.axis_size("dp"))])


def swap(array):
    return lax.ppermute(array, "tensor", [(0, 1), (1, 0)])


class Gather:
    def __init__(self, w_qkv, w_out, w_up, w_down):
        self.n = n = w_up.shape[0]
        self.h = n // 2
        self.pieces = []
        o, u = w_qkv.shape[2], w_up.shape[1]
        self.width = 3 * o
        flat = w_qkv.reshape(3 * n, o)
        wo, wd = w_out.T, w_down.T
        queries = [(flat, slot * n, n, 0, o, slot * o, slot == 2) for slot in range(3)]
        rest = [
            (wo, 0, n, 0, o, 0, False), (w_up, 0, n, 0, 2 * o, o, True),
            (w_up, 0, n, 2 * o, u - 2 * o, 0, False), (wd, 0, n, 0, o, 2 * o, True),
            (wd, 0, n, o, 3 * o, 0, True),
        ]
        self.own, self.q = pack([queries + rest, queries])
        self.e, self.f, self.g = (self.cut(p) for p in (1, 2, 3))

    def cut(self, piece):
        return lax.slice_in_dim(self.own, piece * self.n, (piece + 1) * self.n, axis=0)

    def note(self, array, items, other=0):
        at = 0
        for piece, rel, row, count in items:
            self.pieces.append(Piece(piece * self.width, self.width, rel, row, count, array, at, other))
            at += count

    def part(self, array, at, count):
        return (array, at, count, 0, self.width, 0, True)

    def full(self, piece, *rels):
        return [(piece, rel, 0, self.n) for rel in rels]

    def upper(self, piece, *rels):
        return [(piece, rel, self.h, self.h) for rel in rels]

    def lower(self, piece, *rels):
        return [(piece, rel, 0, self.h) for rel in rels]

    def exchange(self, arrays, after=()):
        fresh = [a for a, _ in arrays if a is not self.own]
        (packed,) = pack([[self.part(a, 0, a.shape[0]) for a, _ in arrays]], fresh=fresh, after=after)
        other = swap(packed)
        self.note(other, [item for _, items in arrays for item in items], 1)
        return packed, other

    def keep(self, got):
        for array, items in got:
            self.note(array, items)
        return got

    def round1(self):
        self.zq = [hop(self.q, k) for k in ZS]
        self.x1, self.y1 = hop(self.own, X), hop(self.own, Y)
        every = range(4)
        got = [(self.own, [i for p in every for i in self.full(p, 0)])]
        got += [(self.x1, [i for p in every for i in self.full(p, X)])]
        got += [(self.y1, [i for p in every for i in self.full(p, Y)])]
        got += [(z, self.full(0, k)) for z, k in zip(self.zq, ZS)]
        self.got1 = self.keep(got)

    def round2(self, after):
        n, h, part = self.n, self.h, self.part
        along = [part(z, 0, n) for z in self.zq]
        xin, yin, e = pack(
            [along + [part(self.y1, h, h)], along + [part(self.x1, 0, h)], [part(self.own, n, n)]],
            fresh=[*self.zq, self.x1, self.y1],
            after=after,
        )
        x, y, self.ze2 = hop(xin, X), hop(yin, Y), hop(e, Z2)
        self.x, self.y = x, y
        self.got2 = self.keep([
            (x, self.full(0, *(X | k for k in ZS)) + self.upper(0, X | Y)),
            (y, self.full(0, *(Y | k for k in ZS)) + self.lower(0, X | Y)),
            (self.ze2, self.full(1, Z2)),
        ])
        return self.exchange(self.got1, [xin])

    def round3(self, after):
        n, h, part = self.n, self.h, self.part
        xin, yin, e, f = pack(
            [
                [part(self.y, i * n + h, h) for i in range(3)] + [part(self.y1, p * n + h, h) for p in (1, 2)],
                [part(self.x, i * n, h) for i in range(3)] + [part(self.x1, p * n, h) for p in (1, 2)],
                [part(self.own, n, n), part(self.ze2, 0, n)],
                [part(self.own, 2 * n, n)],
            ],
            fresh=[self.x, self.y, self.ze2],
            after=after,
        )
        x, y, self.ze1, self.zf2 = hop(xin, X), hop(yin, Y), hop(e, Z1), hop(f, Z2)
        self.x, self.y = x, y
        both = [X | Y | k for k in ZS]
        self.got3 = self.keep([
            (x, self.upper(0, *both) + self.upper(1, X | Y) + self.upper(2, X | Y)),
            (y, self.lower(0, *both) + self.lower(1, X | Y) + self.lower(2, X | Y)),
        ])
        self.late3 = self.keep([(self.ze1, self.full(1, Z1, Z3)), (self.zf2, self.full(2, Z2))])
        return self.exchange(self.got2, [xin])

    def round4(self, after):
        n, h, part = self.n, self.h, self.part
        along = [part(self.ze1, 0, n), part(self.ze2, 0, n), part(self.ze1, n, n)]
        xin, yin, f, g = pack(
            [
                along + [part(self.y1, 3 * n + h, h)],
                along + [part(self.x1, 3 * n, h)],
                [part(self.own, 2 * n, n), part(self.zf2, 0, n)],
                [part(self.own, 3 * n, n)],
            ],
            fresh=[self.ze1, self.zf2],
            after=after,
        )
        x, y, self.zf1, self.zg2 = hop(xin, X), hop(yin, Y), hop(f, Z1), hop(g, Z2)
        self.x, self.y = x, y
        self.got4 = self.keep([
            (x, self.full(1, *(X | k for k in ZS)) + self.upper(3, X | Y)),
            (y, self.full(1, *(Y | k for k in ZS)) + self.lower(3, X | Y)),
            (self.zf1, self.full(2, Z1, Z3)),
            (self.zg2, self.full(3, Z2)),
        ])
        return self.exchange(self.got3, [xin])

    def round5(self, after):
        n, h, part = self.n, self.h, self.part
        along = [part(self.zf1, 0, n), part(self.zf2, 0, n), part(self.zf1, n, n)]
        xin, yin, g, d = pack(
            [
                [part(self.y, i * n + h, h) for i in range(3)] + along,
                [part(self.x, i * n, h) for i in range(3)] + along,
                [part(self.own, 3 * n, n), part(self.zg2, 0, n)],
                [part(self.y, 3 * n, h), part(self.x, 3 * n, h)],
            ],
            fresh=[self.x, self.y, self.zf1, self.zg2],
            after=after,
        )
        self.d = d
        x, y, self.zg1, self.zd2 = hop(xin, X), hop(yin, Y), hop(g, Z1), hop(d, Z2)
        self.x, self.y = x, y
        both = [X | Y | k for k in ZS]
        self.got5 = self.keep([
            (x, self.upper(1, *both) + self.full(2, *(X | k for k in ZS))),
            (y, self.lower(1, *both) + self.full(2, *(Y | k for k in ZS))),
            (self.zg1, self.full(3, Z1, Z3)),
            (self.zd2, self.full(3, X | Y | Z2)),
        ])
        return self.exchange(self.late3 + self.got4, [xin])

    def round6(self, after):
        n, h, part = self.n, self.h, self.part
        along = [part(self.zg1, 0, n), part(self.zg2, 0, n), part(self.zg1, n, n)]
        xin, yin, d = pack(
            [
                [part(self.y, 3 * h + i * n + h, h) for i in range(3)] + along,
                [part(self.x, 3 * h + i * n, h) for i in range(3)] + along,
                [part(self.d, 0, n), part(self.zd2, 0, n)],
            ],
            fresh=[self.x, self.y, self.zg1, self.zd2],
            after=after,
        )
        x, y, zd1 = hop(xin, X), hop(yin, Y), hop(d, Z1)
        both = [X | Y | k for k in ZS]
        self.got6 = self.keep([
            (x, self.upper(2, *both) + self.full(3, *(X | k for k in ZS))),
            (y, self.lower(2, *both) + self.full(3, *(Y | k for k in ZS))),
            (zd1, self.full(3, X | Y | Z1, X | Y | Z3)),
        ])
        return self.exchange(self.got5, [xin])

    def last(self, after):
        return self.exchange(self.got6, after)


class GatherPlain:
    def __init__(self, w_qkv, w_out, w_up, w_down):
        local = jnp.concatenate([w_qkv[0], w_qkv[1], w_qkv[2], w_out.T, w_up, w_down.T], axis=1)
        rows, width = local.shape
        whole = lax.all_gather(local, ("dp", "tensor")).reshape(lax.axis_size("dp"), 2, rows, width)
        self.pieces = [Piece(0, width, None, 0, 0, whole, 0, other) for other in range(2)]

    def round1(self):
        return None

    def round2(self, after):
        return None, None

    round3 = round4 = round5 = round6 = last = round2


class Spot:
    def __init__(self, array, row, rows, col, cols):
        self.array, self.row, self.rows, self.col, self.cols = array, row, rows, col, cols

    def of(self, ref, me, t):
        at = lambda v, unit: pl.multiple_of(v(me, t), unit) if callable(v) else v
        return ref.at[pl.ds(at(self.row, 16), self.rows), pl.ds(at(self.col, 128), self.cols)]


def arrange(where, shapes, moves, fresh=(), after=()):
    arrays = []
    for source, _, _ in moves:
        if not any(a is source.array for a in arrays):
            arrays.append(source.array)
    used = len(arrays)
    arrays += [a for a in after if a is not None]
    near = [any(a is f for f in fresh) for a in arrays]
    number = lambda array: next(i for i, a in enumerate(arrays) if a is array)
    plan = [(number(source.array), source, out, target) for source, out, target in moves]

    def kernel(where_ref, *refs):
        ins, results, sems = refs[: len(arrays)], refs[len(arrays) : -1], refs[-1]
        me, t = where_ref[0], where_ref[1]
        copies = []
        for index, (slot, source, out, target) in enumerate(plan):
            copy = pltpu.make_async_copy(
                source.of(ins[slot], me, t), target.of(results[out], me, t), sems.at[index]
            )
            copy.start()
            copies.append(copy)
        for copy in copies:
            copy.wait()

    spaces = [pltpu.VMEM if n else pltpu.HBM for n in near]
    return pl.pallas_call(
        kernel,
        in_specs=[pl.BlockSpec(memory_space=pltpu.SMEM)] + [pl.BlockSpec(memory_space=m) for m in spaces],
        out_specs=[pl.BlockSpec(memory_space=pltpu.VMEM)] * len(shapes),
        out_shape=[pltpu.VMEM(shape, BF) for shape in shapes],
        scratch_shapes=[pltpu.SemaphoreType.DMA((len(plan),))],
        compiler_params=pltpu.CompilerParams(vmem_limit_bytes=8 * 2**20),
        cost_estimate=pl.CostEstimate(
            flops=0, bytes_accessed=sum(h * w * 4 for h, w in shapes), transcendentals=0
        ),
    )(where, *[pltpu.with_memory_space_constraint(a, m) for a, m in zip(arrays, spaces)])


class GradientSum:
    def __init__(self, where, arrays, mine, rank, adapters):
        self.where, self.arrays = where, arrays
        self.mine, self.rank, self.adapters = mine, rank, adapters
        self.rows = mine * rank
        self.widths = [a.shape[1] for a in arrays]
        self.starts = [sum(self.widths[:i]) for i in range(len(arrays))]
        self.total = sum(self.widths)
        self.chunk = self.total // 8

    def cores(self, after=()):
        half = self.total // 2
        moves = [
            (
                Spot(a, 0, self.rows, lambda me, t, w=w: (1 - t) * (w // 2), w // 2),
                0,
                Spot(None, 0, self.rows, s // 2, w // 2),
            )
            for a, w, s in zip(self.arrays, self.widths, self.starts)
        ]
        (out,) = arrange(self.where, [(self.rows, half)], moves, after=after)
        self.other = swap(out)
        return out

    def plane(self, after=()):
        moves = []
        for k in range(4):
            for a, w, s in zip(self.arrays, self.widths, self.starts):
                e = w // 8
                moves.append((
                    Spot(a, 0, self.rows, lambda me, t, e=e, k=k: (t * 4 + ((me & 3) ^ k)) * e, e),
                    k,
                    Spot(None, 0, self.rows, s // 8, e),
                ))
                moves.append((
                    Spot(self.other, 0, self.rows, lambda me, t, e=e, s=s, k=k: s // 2 + ((me & 3) ^ k) * e, e),
                    k,
                    Spot(None, self.rows, self.rows, s // 8, e),
                ))
        outs = arrange(self.where, [(2 * self.rows, self.chunk)] * 4, moves, fresh=[self.other], after=after)
        self.parts = [outs[0], hop(outs[1], X), hop(outs[2], Y), hop(outs[3], X | Y)]
        return outs[0]

    def fold(self, after=()):
        rank, chunk, count = self.rank, self.chunk, 2 * self.mine
        quarter = self.adapters * rank // 4
        after = [a for a in after if a is not None]

        def kernel(where_ref, *refs):
            ins, outs, total = refs[:4], refs[4 + len(after) : 8 + len(after)], refs[-1]
            z = where_ref[0] // 4
            total[...] = jnp.zeros_like(total)
            for k in range(4):
                for index in range(count):
                    pick = where_ref[2 + k * count + index]
                    into = pl.ds(pl.multiple_of(pick * rank, rank), rank)
                    total[into, :] += ins[k][index * rank : (index + 1) * rank, :].astype(F32)
            for k in range(4):
                rows = pl.ds(pl.multiple_of((z ^ k) * quarter, quarter), quarter)
                outs[k][...] = total[rows, :].astype(BF)

        outs = self.local(kernel, self.parts, after, [(quarter, chunk)] * 4, [(self.adapters * rank, chunk)])
        self.parts = [outs[0]] + [hop(outs[k], 4 * k) for k in (1, 2, 3)]
        return outs[0]

    def local(self, kernel, arrays, after, shapes, scratch):
        vmem = pl.BlockSpec(memory_space=pltpu.VMEM)
        return pl.pallas_call(
            kernel,
            in_specs=[pl.BlockSpec(memory_space=pltpu.SMEM)]
            + [vmem] * len(arrays)
            + [pl.BlockSpec(memory_space=pltpu.HBM)] * len(after),
            out_specs=[vmem] * len(shapes),
            out_shape=[pltpu.VMEM(shape, BF) for shape in shapes],
            scratch_shapes=[pltpu.VMEM(shape, F32) for shape in scratch],
            compiler_params=pltpu.CompilerParams(vmem_limit_bytes=12 * 2**20),
            cost_estimate=pl.CostEstimate(
                flops=0, bytes_accessed=sum(h * w * 8 for h, w in shapes), transcendentals=0
            ),
        )(
            self.where,
            *[pltpu.with_memory_space_constraint(a, pltpu.VMEM) for a in arrays],
            *[in_hbm(a) for a in after],
        )

    def depth(self, after=()):
        after = [a for a in after if a is not None]

        def kernel(where_ref, *refs):
            total = refs[0][...].astype(F32)
            for ref in refs[1:4]:
                total += ref[...].astype(F32)
            refs[-1][...] = total.astype(BF)

        (out,) = self.local(kernel, self.parts, after, [self.parts[0].shape], [])
        self.parts = [out] + [hop(out, 4 * k) for k in (1, 2, 3)]
        return out

    def back(self, after=()):
        quarter = self.adapters * self.rank // 4
        moves = [
            (
                Spot(self.parts[k], 0, quarter, 0, self.chunk),
                0,
                Spot(None, lambda me, t, k=k: ((me >> 2) ^ k) * quarter, quarter, 0, self.chunk),
            )
            for k in range(4)
        ]
        tall = self.adapters * self.rank
        (out,) = arrange(self.where, [(tall, self.chunk)], moves, fresh=self.parts, after=after)
        self.parts = [out, hop(out, X), hop(out, Y), hop(out, X | Y)]
        return out

    def give(self, after=()):
        tall = self.adapters * self.rank
        moves = [
            (Spot(part, 0, tall, 0, self.chunk), 0, Spot(None, k * tall, tall, 0, self.chunk))
            for k, part in enumerate(self.parts)
        ]
        (out,) = arrange(self.where, [(4 * tall, self.chunk)], moves, fresh=self.parts, after=after)
        self.theirs = swap(out)
        self.ours = out
        return out


def finish(where, sums, results, after=()):
    tall = sums[0].adapters * sums[0].rank
    after = [a for a in after if a is not None]
    inputs = [a for s in sums for a in (s.ours, s.theirs)]

    def kernel(where_ref, *refs):
        outs = refs[len(inputs) + len(after) :]
        me, t = where_ref[0], where_ref[1]
        for out, parts in zip(outs, results):
            for place, (number, which) in enumerate(parts):
                total = sums[number]
                start, width = total.starts[which] // 8, total.widths[which] // 8
                for core in range(2):
                    for k in range(4):
                        column = ((t ^ core) * 4 + ((me & 3) ^ k)) * width
                        out[place * tall : (place + 1) * tall, pl.ds(pl.multiple_of(column, 128), width)] = refs[
                            2 * number + core
                        ][k * tall : (k + 1) * tall, start : start + width].astype(F32)

    vmem = pl.BlockSpec(memory_space=pltpu.VMEM)
    shapes = [(len(parts) * tall, sums[parts[0][0]].widths[parts[0][1]]) for parts in results]
    return pl.pallas_call(
        kernel,
        in_specs=[pl.BlockSpec(memory_space=pltpu.SMEM)]
        + [vmem] * len(inputs)
        + [pl.BlockSpec(memory_space=pltpu.HBM)] * len(after),
        out_specs=[vmem] * len(results),
        out_shape=[jax.ShapeDtypeStruct(shape, F32) for shape in shapes],
        compiler_params=pltpu.CompilerParams(vmem_limit_bytes=32 * 2**20),
        cost_estimate=pl.CostEstimate(
            flops=0, bytes_accessed=sum(h * w * 6 for h, w in shapes), transcendentals=0
        ),
    )(where, *inputs, *[in_hbm(a) for a in after])


def shards(
    hidden_in, segment_ids, adapter_pick, w_qkv, w_out, w_up, w_down, ln_gain, ln_bias,
    adapt_a, adapt_b, up_a, up_b, down_a, down_b, grad_out,
):
    dp = lax.axis_size("dp")
    t = lax.axis_index("tensor")
    block, ff_half = w_up.shape
    width = hidden_in.shape[2]
    half = width // 2
    ff = 2 * ff_half
    positions = hidden_in.shape[1]
    length = 2 * positions
    mine = hidden_in.shape[0] // 2
    rank = adapt_b.shape[2]
    adapters = adapt_b.shape[1]

    def to_sequences(piece):
        there = swap(lax.dynamic_slice_in_dim(piece, mine * (1 - t), mine, 0))
        here = lax.dynamic_slice_in_dim(piece, mine * t, mine, 0)
        low = jnp.where(t == 0, here, there)
        high = jnp.where(t == 0, there, here)
        return jnp.concatenate([low, high], axis=1)

    def to_positions(value):
        here = lax.dynamic_slice_in_dim(value, positions * t, positions, 1)
        there = swap(lax.dynamic_slice_in_dim(value, positions * (1 - t), positions, 1))
        low = jnp.where(t == 0, here, there)
        high = jnp.where(t == 0, there, here)
        return jnp.concatenate([low, high], axis=0)

    gather = (Gather if dp == 16 else GatherPlain)(w_qkv, w_out, w_up, w_down)
    gather.round1()
    x, cotangent = to_sequences(hidden_in), to_sequences(grad_out)
    def columns(first, count):
        return (gather.pieces, first, count, dp, block)

    qkv_w = columns(0, 3 * half)
    out_w = columns(3 * half, half)
    part = 2 * half
    up_parts = [columns(4 * half + p, part) for p in range(0, ff_half, part)]
    up_w = columns(4 * half, ff_half)
    down_w = columns(4 * half + ff_half, ff_half)

    segs = lax.dynamic_slice_in_dim(segment_ids, mine * t, mine, 0)
    pick = lax.dynamic_slice_in_dim(adapter_pick, mine * t, mine, 0)
    meta = jnp.concatenate([pick, jnp.stack([lax.axis_index("dp"), t]).astype(pick.dtype)])
    if dp == 16:
        ordered = jnp.where(t == 0, adapter_pick, jnp.roll(adapter_pick, -mine))
        plane = [ordered, hop(ordered, X), hop(ordered, Y), hop(ordered, X | Y)]
        where = jnp.concatenate([meta[mine:], *plane])
    seg_col = segs.reshape(mine, length, 1)
    seg_row = segs.reshape(mine, 1, length)
    a_t = jnp.swapaxes(adapt_a, 2, 3)
    ua_t = jnp.swapaxes(up_a, 1, 2)
    da_t = jnp.swapaxes(down_a, 1, 2)

    _, met = gather.round2([x, cotangent, meta, seg_col, seg_row])
    _, met = gather.round3([met])
    gate, _ = gather.round4([met])
    tokens = mine * length
    seq3 = lambda s, m: (s, 0, 0)
    seq4 = lambda s, m: (s, 0, 0, 0)
    fixed2 = lambda s, m: (0, 0)
    picked3 = lambda s, m: (m[s], 0, 0)
    slots4 = lambda s, m: (0, m[s], 0, 0)
    last4 = lambda s, m: (3, m[s], 0, 0)
    row = lambda a: (a, (1, *a.shape[1:]), seq3 if a.ndim == 3 else seq4)
    whole = lambda a: (a, a.shape, fixed2)
    factor = lambda a: (a, (1, *a.shape[1:]), picked3)
    slots = lambda a: (a, (a.shape[0], 1, *a.shape[2:]), slots4)
    last = lambda a: (a, (1, 1, *a.shape[2:]), last4)
    made = lambda dtype, *shape: ((mine, *shape), dtype, (1, *shape), seq3 if len(shape) == 2 else seq4)

    qkv, rank_qkv = call(
        qkv_kernel, meta,
        [row(x), slots(a_t), slots(adapt_b)],
        [made(BF, 3, length, width), made(BF, length, 3 * rank)],
        6 * tokens * width * width,
        weights=[qkv_w],
        after=[gate],
        limit=28 * 2**20,
    )
    gate, met = gather.round5([qkv])

    groups = width // GROUP

    def heads_of(slot, first=0):
        return pl.BlockSpec((1, 1, length, GROUP), lambda s, h: (s + first, slot, 0, h))

    def seg_specs(first=0):
        return [
            pl.BlockSpec((1, length, 1), lambda s, h: (s + first, 0, 0)),
            pl.BlockSpec((1, 1, length), lambda s, h: (s + first, 0, 0)),
        ]

    lse_spec = pl.BlockSpec((1, 1, 8, length), lambda s, h: (s, h, 0, 0))
    heads_spec = pl.BlockSpec((1, length, GROUP), lambda s, h: (s, 0, h))

    def attend(first, after):
        after = [a for a in after if a is not None]

        def body(q, k, v, sc, sr, *refs):
            attend_kernel(q, k, v, sc, sr, *refs[len(after) :])

        return pl.pallas_call(
            body,
            grid=(1, groups),
            in_specs=[heads_of(j, first) for j in range(3)]
            + seg_specs(first)
            + [pl.BlockSpec(memory_space=pltpu.HBM) for _ in after],
            out_specs=[heads_spec, lse_spec],
            out_shape=[
                pltpu.HBM((1, length, width), BF),
                pltpu.HBM((1, groups, 8, length), F32),
            ],
            **params(16 * length * length * width, length * width * 8, 24 * 2**20),
        )(*[in_hbm(a) for a in [qkv, qkv, qkv, seg_col, seg_row, *after]])

    attended = []
    for index in range(mine):
        attended.append(attend(index, [gate]))
        gate = attended[-1][1]
    gate, _ = gather.round6([gate, met])
    attention = jnp.concatenate([a for a, _ in attended], axis=0)
    lse = jnp.concatenate([a for _, a in attended], axis=0)

    normed, inverse, middle_low, rank_out = call(
        out_kernel, meta,
        [row(attention), row(x), last(a_t), last(adapt_b), whole(ln_gain), whole(ln_bias)],
        [made(F32, length, width), made(F32, length, 128), made(BF, length, width), made(BF, length, rank)],
        2 * tokens * width * width,
        scratch=[pltpu.VMEM((length, width), F32)],
        weights=[out_w],
        limit=28 * 2**20,
        after=[gate],
    )

    gate, _ = gather.last([rank_out])
    acts, slopes, rank_up = [], [], None
    for index, weight in enumerate(up_parts):
        blocks = ff_half // part
        up_cols = [
            (up_b, (1, rank, part), lambda s, m, at=h * blocks + index: (m[s], 0, at)) for h in range(2)
        ]
        act, slope, rank_up = call(
            up_kernel, meta,
            [row(middle_low), factor(ua_t), *up_cols],
            [made(BF, length, 2 * part), made(BF, length, 2 * part), made(BF, length, rank)],
            4 * tokens * width * part * 2,
            weights=[weight],
            limit=36 * 2**20,
            after=[gate],
        )
        gate = rank_up
        acts.append(act)
        slopes.append(slope)

    layer_out, second, grad_hidden, g_down_a, g_down_b = call(
        down_kernel, meta,
        [row(normed), row(cotangent), factor(da_t), factor(down_b), whole(ln_gain), whole(ln_bias),
         *[row(a) for a in acts], *[row(a) for a in slopes]],
        [made(BF, length, width), made(F32, length, width), made(BF, length, ff),
         made(BF, rank, ff), made(BF, rank, width)],
        4 * tokens * width * ff,
        scratch=[pltpu.VMEM((length, width), F32), pltpu.VMEM((length, width), BF)],
        weights=[down_w],
    )

    grad_first, grad_att, g_up_a, g_up_b, g_out_a, g_out_b = call(
        mlp_back_kernel, meta,
        [row(grad_hidden), row(middle_low), row(normed), row(inverse), row(second), row(attention),
         row(rank_up), row(rank_out), factor(ua_t), factor(up_b), last(a_t), last(adapt_b),
         whole(ln_gain)],
        [made(F32, length, width), made(BF, length, width), made(BF, rank, width),
         made(BF, rank, ff), made(BF, rank, width), made(BF, rank, width)],
        2 * tokens * width * (ff + width),
        scratch=[pltpu.VMEM((length, width), F32), pltpu.VMEM((length, width), BF)],
        weights=[up_w, out_w],
    )

    flat = lambda g: g.reshape(mine * rank, g.shape[-1])
    seqs = [g_down_a, g_down_b, g_up_a, g_up_b, g_out_a, g_out_b]
    fast = dp == 16
    if fast:
        first_sum = GradientSum(where, [flat(g) for g in seqs], mine, rank, adapters)
        gate = first_sum.cores()
    else:
        gate = None

    def attend_back(first, after):
        after = [a for a in after if a is not None]

        def body(q, k, v, sc, sr, l, o, do, *refs):
            attend_back_kernel(q, k, v, sc, sr, l, o, do, *refs[len(after) :])

        from_seq = pl.BlockSpec((1, length, GROUP), lambda s, h: (s + first, 0, h))
        args = [qkv, qkv, qkv, seg_col, seg_row, attended[first][1], attended[first][0], grad_att, *after]
        return pl.pallas_call(
            body,
            grid=(1, groups),
            in_specs=[heads_of(j, first) for j in range(3)]
            + seg_specs(first)
            + [lse_spec, heads_spec, from_seq]
            + [pl.BlockSpec(memory_space=pltpu.HBM) for _ in after],
            out_specs=[heads_spec] * 3,
            out_shape=[pltpu.HBM((1, length, width), BF)] * 3,
            **params(40 * length * length * width, length * width * 16, 32 * 2**20),
        )(*[in_hbm(a) for a in args])

    grads_qkv = []
    for index in range(mine):
        grads_qkv.append(attend_back(index, [gate]))
        gate = grads_qkv[-1][0]
        if fast and index == 0:
            gate = first_sum.plane([gate])
    if fast:
        gate = first_sum.fold([gate])

    one3 = lambda s, m: (0, 0, 0)

    def per_sequence(index, meta_at):
        own = [(g, (1, length, width), one3) for g in grads_qkv[index]]
        pick_row = lambda a: (a, (1, *a.shape[1:]), lambda s, m: (index, *([0] * (a.ndim - 1))))
        pick_slots = lambda a: (a, (a.shape[0], 1, *a.shape[2:]), lambda s, m: (0, m[s], 0, 0))
        return own, pick_row, pick_slots

    def one(dtype, *shape):
        return ((1, *shape), dtype, (1, *shape), one3)

    metas = [jnp.concatenate([meta[i : i + 1], meta[mine:]]) for i in range(mine)]
    ranked = []
    for index in range(mine):
        own, pick_row, pick_slots = per_sequence(index, metas[index])
        ranked.append(call(
            rank_back_kernel, metas[index],
            own + [pick_row(x), pick_row(rank_qkv), pick_slots(adapt_b)],
            [one(BF, 3 * rank, length)] + [one(BF, rank, width)] * 6,
            18 * length * width * rank,
            after=[gate],
            limit=32 * 2**20,
        ))
        gate = ranked[-1][0]
    later = [jnp.concatenate([r[1 + j] for r in ranked], axis=0) for j in range(6)]
    if fast:
        second_sum = GradientSum(where, [flat(g) for g in later], mine, rank, adapters)
        gate = second_sum.cores([gate])
        gate = first_sum.depth([gate])

    grad_ins = []
    for index in range(mine):
        own, pick_row, pick_slots = per_sequence(index, metas[index])
        (piece,) = call(
            qkv_back_kernel, metas[index],
            own + [(ranked[index][0], (1, 3 * rank, length), one3), pick_row(grad_first), pick_slots(a_t)],
            [one(F32, length, width)],
            6 * length * width * width,
            weights=[qkv_w],
            after=[gate],
            limit=32 * 2**20,
        )
        grad_ins.append(piece)
        gate = piece
        if fast and index == 0:
            gate = second_sum.plane([gate])
            gate = first_sum.back([gate])
    grad_in = jnp.concatenate(grad_ins, axis=0)
    turned = lambda v: jnp.swapaxes(v, -1, -2)
    if fast:
        gate = second_sum.fold([gate])
        gate = first_sum.give([gate])
        gate = second_sum.depth([gate])
        done1 = finish(where, [first_sum], [[(0, 0)], [(0, 1)], [(0, 2)], [(0, 3)]], [gate])
        gate = second_sum.back([done1[0]])
        second_sum.give([gate])
        all_a, all_b = finish(
            where, [second_sum, first_sum],
            [[(0, 0), (0, 1), (0, 2), (1, 4)], [(0, 3), (0, 4), (0, 5), (1, 5)]],
        )
        shaped = lambda v: v.reshape(-1, adapters, rank, v.shape[1])
        da, db, ua, ub = (shaped(v)[0] for v in done1)
        return (
            to_positions(layer_out), to_positions(grad_in),
            turned(shaped(all_a)), shaped(all_b), turned(ua), ub, turned(da), db,
        )

    onehot = (pick[:, None] == jnp.arange(adapters)[None, :]).astype(F32)

    def fold(per_sequence):
        total = onehot[0][:, None, None] * per_sequence[0][None].astype(F32)
        for index in range(1, mine):
            total += onehot[index][:, None, None] * per_sequence[index][None].astype(F32)
        return total

    sums = lax.psum(
        tuple(fold(g) for g in [*later[:3], g_out_a, *later[3:], g_out_b, g_up_a, g_up_b, g_down_a, g_down_b]),
        ("dp", "tensor"),
    )
    return (
        to_positions(layer_out),
        to_positions(grad_in),
        turned(jnp.stack(sums[:4])),
        jnp.stack(sums[4:8]),
        turned(sums[8]),
        sums[9],
        turned(sums[10]),
        sums[11],
    )


def solution(mesh):
    placed = (
        P("dp", "tensor", None),
        P("dp", None),
        P("dp"),
        P(None, "dp", "tensor"),
        P("tensor", "dp"),
        P("dp", "tensor"),
        P("tensor", "dp"),
        P(),
        P(),
        P(),
        P(),
        P(),
        P(),
        P(),
        P(),
        P("dp", "tensor", None),
    )
    return jax.shard_map(
        shards,
        mesh=mesh,
        in_specs=placed,
        out_specs=(P("dp", "tensor", None), P("dp", "tensor", None), P(), P(), P(), P(), P(), P()),
        check_vma=False,
    )
```

time: 906 us -> 461 us (0.51)
  matrix products: 365 us -> 0 us
  waiting for transfers between devices: 371 us -> 58.5 us
  Pallas kernels: 0 us -> 272 us
  starting transfers between devices: 0.52 us -> 66.8 us
  other arithmetic: 93.8 us -> 28.3 us
  local copies, waits for them, and re-layouts: 49.8 us -> 29 us
  between operations: 15 us -> 2.07 us
    dot_general x100 -> x0, matrix products: 365 us -> none  [the longest x6 59.8 us: project_back(): jnp.einsum('snr,sdr->snd', grad_rank, factor_one.astype(jnp.float32), pre...]
    pallas_call x0 -> x40, Pallas kernels: none -> 272 us  [the longest x10 187 us: call(): pl.pallas_call(body, grid_spec=pltpu.PrefetchScalarGridSpec(num_scalar_pr...]
    all_gather x8 -> x0, waiting for transfers between devices: 171 us -> none  [the longest x1 71.1 us: shards(): lax.all_gather(w_up, 'dp', axis=0, tiled=True)]
    psum x1 -> x0, waiting for transfers between devices: 145 us -> none  [shards(): lax.psum((jnp.stack(folded_one), jnp.stack(folded_two), fold_rows(onehot_...]
    ppermute x0 -> x64, starting transfers between devices: none -> 66.8 us  [the longest x50 65.1 us: hop(): lax.ppermute(array, 'dp', [(i, i ^ bits) for i in range(lax.axis_size('dp...]
    ppermute x0 -> x64, waiting for transfers between devices: none -> 58.5 us  [the longest x50 58.1 us: hop(): lax.ppermute(array, 'dp', [(i, i ^ bits) for i in range(lax.axis_size('dp...]
    convert_element_type x8 -> x0, other arithmetic: 57 us -> none  [the longest x1 39.8 us: shards(): jax.nn.gelu(hidden_units, approximate=False).astype(jnp.bfloat16)]
    reduce_scatter x4 -> x0, waiting for transfers between devices: 51 us -> none  [the longest x1 18.1 us: shards(): lax.psum_scatter(grad_mlp_part, 'tensor', scatter_dimension=1, tiled=True)]
  transfers between devices with their start and end apart: 13 -> 64, of which waited for: 10 -> 15; matrix products, arithmetic and copies ran while one was open for 30% -> 7% of each run, Pallas kernels for 0% -> 32%
where the time goes in v2:
time: 461 us; the launch traced here: 456 us
  Pallas kernels  272 us (59%)
  starting transfers between devices  66.8 us (14%)
  waiting for transfers between devices  58.5 us (13%)
  local copies, waits for them, and re-layouts  29 us (6%)
  other arithmetic  28.3 us (6%)
    pallas_call x10, Pallas kernels, call(): pl.pallas_call(body, grid_spec=pltpu.PrefetchScalarGridSpec(num_scalar_pr...  187 us
    ppermute x50, starting transfers between devices, hop(): lax.ppermute(array, 'dp', [(i, i ^ bits) for i in range(lax.axis_size('dp...  65.1 us
    ppermute x50, waiting for transfers between devices, hop(): lax.ppermute(array, 'dp', [(i, i ^ bits) for i in range(lax.axis_size('dp...  58.1 us
    pallas_call x2, Pallas kernels, attend_back(): pl.pallas_call(body, grid=(1, groups), in_specs=[heads_of(j, first) for j...  30.9 us
    unnamed x163, local copies, waits for them, and re-layouts  22 us
    pallas_call x2, Pallas kernels, attend(): pl.pallas_call(body, grid=(1, groups), in_specs=[heads_of(j, first) for j...  20.5 us
    pallas_call x8, Pallas kernels, arrange(): pl.pallas_call(kernel, in_specs=[pl.BlockSpec(memory_space=pltpu.SMEM)] +...  12.3 us
    pallas_call x12, Pallas kernels, pack(): pl.pallas_call(kernel, in_specs=[pl.BlockSpec(memory_space=space) for spa...  12 us
  transfers between devices with their start and end apart: 64, of which 15 were waited for; matrix products, arithmetic and copies ran while one was open for 7% of the time, Pallas kernels for 32%

profile of v2, /device:TPU:0, one launch (start us, length us, event | category | flops | bytes accessed | tf_op | source)
XLA Modules:
  0.0 456.3 jit_solution(489087750774997568)
XLA Ops:
  6.0 3.0 collective-permute-start.2
  10.5 3.6 collective-permute-start.5
  22.7 7.7 %collective-permute-done.4.refs_1_.refs_4_.refs_7_.refs_10_ = bf16[64,1536]{1,0:T(8,128)(2,1)S(1)} collective-permute-done((bf16[64,1536]{1,0:T(8,128)(2,1)S(1)}, bf16[64,1536]{1,0:T(8,128)(2,1)S(1)}, u32[]{:S(2)}, u32[]{:S(2)}) %collective-permute-start.4) | collective-permute-done | bytes 196640 | tf_op jit(solution)/shard_map/ppermute | solution.py:494
  36.3 10.4 %collective-permute-done.10.refs_5_.refs_2_.refs_1_.refs_9_.refs_7_.refs_16_.refs_37_ = bf16[64,1536]{1,0:T(8,128)(2,1)S(1)} collective-permute-done((bf16[64,1536]{1,0:T(8,128)(2,1)S(1)}, bf16[64,1536]{1,0:T(8,128)(2,1)S(1)}, u32[]{:S(2)}, u32[]{:S(2)}) %collective-permute-start.10) | collective-permute-done | bytes 196640 | tf_op jit(solution)/shard_map/ppermute | solution.py:494
  46.7 5.1 %collective-permute-done.8.refs_0_.refs_1_.refs_10_.refs_13_ = bf16[224,1536]{1,0:T(8,128)(2,1)S(1)} collective-permute-done((bf16[224,1536]{1,0:T(8,128)(2,1)S(1)}, bf16[224,1536]{1,0:T(8,128)(2,1)S(1)}, u32[]{:S(2)}, u32[]{:S(2)}) %collective-permute-start.8) | collective-permute-done | bytes 688160 | tf_op jit(solution)/shard_map/ppermute | solution.py:494
  58.3 2.8 collective-permute-start.15
  61.1 9.9 %collective-permute-done.15.refs_5_.refs_2_.refs_1_.refs_10_.refs_16_.refs_21_ = bf16[64,1536]{1,0:T(8,128)(2,1)S(1)} collective-permute-done((bf16[64,1536]{1,0:T(8,128)(2,1)S(1)}, bf16[64,1536]{1,0:T(8,128)(2,1)S(1)}, u32[]{:S(2)}, u32[]{:S(2)}) %collective-permute-start.15) | collective-permute-done | bytes 196640 | tf_op jit(solution)/shard_map/ppermute | solution.py:494
  83.7 17.8 %shard_map.222 = (bf16[2,3,512,1024]{3,2,1,0:T(8,128)(2,1)}, bf16[2,512,48]{2,1,0:T(8,128)(2,1)}) custom-call(s32[4]{0:T(128)S(1)} %copy-done.60, bf16[2,512,1024]{2,1,0:T(8,128)(2,1)} %pad_maximum_fusion.1.refs_6_.refs_0_.refs_1_.refs_3_, bf16[4,8,16,1024]{3,2,1,0:T(8,128)(2,1)} %bitcast.34, bf16[4,8,16,1024]{3,2,1,0:T(8,128)(2,1)} %refs_5_.7, ...), custom_call_target="tpu_custom_call" | custom-call | flops 6442450944 | bytes 16875520 | tf_op jit(solution)/shard_map/pallas_call | solution.py:412
  108.4 10.2 %shard_map.225 = (bf16[1,512,1024]{2,1,0:T(8,128)(2,1)}, f32[1,4,8,512]{3,2,1,0:T(8,128)}) custom-call(bf16[2,3,512,1024]{3,2,1,0:T(8,128)(2,1)} %get-tuple-element.107.refs_6_.q.k.v, bf16[2,3,512,1024]{3,2,1,0:T(8,128)(2,1)} %get-tuple-element.107.refs_6_.q.k.v, bf16[2,3,512,1024]{3,2,1,0:T(8,128)(2,1)} %get-tuple-element.107.refs_6_.q.k.v, ...), custom_call_target="tpu_custom_call" | custom-call | flops 4294967296 | bytes 4194304 | tf_op jit(solution)/shard_map/pallas_call | solution.py:1001
  118.6 10.2 %shard_map.226 = (bf16[1,512,1024]{2,1,0:T(8,128)(2,1)}, f32[1,4,8,512]{3,2,1,0:T(8,128)}) custom-call(bf16[2,3,512,1024]{3,2,1,0:T(8,128)(2,1)} %get-tuple-element.107.refs_6_.q.k.v, bf16[2,3,512,1024]{3,2,1,0:T(8,128)(2,1)} %get-tuple-element.107.refs_6_.q.k.v, bf16[2,3,512,1024]{3,2,1,0:T(8,128)(2,1)} %get-tuple-element.107.refs_6_.q.k.v, ...), custom_call_target="tpu_custom_call" | custom-call | flops 4294967296 | bytes 4194304 | tf_op jit(solution)/shard_map/pallas_call | solution.py:1001
  139.8 11.8 %shard_map.229 = (f32[2,512,1024]{2,1,0:T(8,128)}, f32[2,512,128]{2,1,0:T(8,128)}, bf16[2,512,1024]{2,1,0:T(8,128)(2,1)}, bf16[2,512,16]{2,1,0:T(8,128)(2,1)}) custom-call(s32[4]{0:T(128)S(1)} %copy-done.60, bf16[2,512,1024]{2,1,0:T(8,128)(2,1)} %copy-done.68, bf16[2,512,1024]{2,1,0:T(8,128)(2,1)} %pad_maximum_fusion.1.refs_6_.refs_0_.refs_1_.refs_3_, ...), custom_call_target="tpu_custom_call" | custom-call | flops 2147483648 | bytes 15253504 | tf_op jit(solution)/shard_map/pallas_call | solution.py:412
  151.6 3.4 collective-permute-done.28.refs_1_.refs_17_.refs_28_.refs_31_
  164.3 17.7 %shard_map.231 = (bf16[2,512,2048]{2,1,0:T(8,128)(2,1)}, bf16[2,512,2048]{2,1,0:T(8,128)(2,1)}, bf16[2,512,16]{2,1,0:T(8,128)(2,1)}) custom-call(s32[4]{0:T(128)S(1)} %copy-done.60, bf16[2,512,1024]{2,1,0:T(8,128)(2,1)} %get-tuple-element.121.refs_0_.refs_1_, bf16[8,16,1024]{2,1,0:T(8,128)(2,1)} %bitcast.56, bf16[8,16,4096]{2,1,0:T(8,128)(2,1)} %refs_9_.1, ...), custom_call_target="tpu_custom_call" | custom-call | flops 8589934592 | bytes 17072128 | tf_op jit(solution)/shard_map/pallas_call | solution.py:412
  183.4 17.7 %shard_map.232 = (bf16[2,512,2048]{2,1,0:T(8,128)(2,1)}, bf16[2,512,2048]{2,1,0:T(8,128)(2,1)}, bf16[2,512,16]{2,1,0:T(8,128)(2,1)}) custom-call(s32[4]{0:T(128)S(1)} %copy-done.60, bf16[2,512,1024]{2,1,0:T(8,128)(2,1)} %get-tuple-element.121.refs_0_.refs_1_, bf16[8,16,1024]{2,1,0:T(8,128)(2,1)} %bitcast.57, bf16[8,16,4096]{2,1,0:T(8,128)(2,1)} %refs_9_.1, ...), custom_call_target="tpu_custom_call" | custom-call | flops 8589934592 | bytes 17072128 | tf_op jit(solution)/shard_map/pallas_call | solution.py:412
  201.1 56.5 %shard_map.233 = (bf16[2,512,1024]{2,1,0:T(8,128)(2,1)}, f32[2,512,1024]{2,1,0:T(8,128)}, bf16[2,512,4096]{2,1,0:T(8,128)(2,1)}, bf16[2,16,4096]{2,1,0:T(8,128)(2,1)}, bf16[2,16,1024]{2,1,0:T(8,128)(2,1)}) custom-call(s32[4]{0:T(128)} %pad_add_fusion.refs_8_.meta_ref, f32[2,512,1024]{2,1,0:T(8,128)} %get-tuple-element.120.refs_0_.refs_2_, ...), custom_call_target="tpu_custom_call" | custom-call | flops 17179869184 | bytes 47792128 | tf_op jit(solution)/shard_map/pallas_call | solution.py:412
  257.7 35.1 %shard_map.234 = (f32[2,512,1024]{2,1,0:T(8,128)}, bf16[2,512,1024]{2,1,0:T(8,128)(2,1)}, bf16[2,16,1024]{2,1,0:T(8,128)(2,1)}, bf16[2,16,4096]{2,1,0:T(8,128)(2...) custom-call(s32[4]{0:T(128)} %pad_add_fusion.refs_8_.meta_ref, ...), custom_call_target="tpu_custom_call" | custom-call | flops 10737418240 | bytes 42213376 | tf_op jit(solution)/shard_map/pallas_call | solution.py:412
  295.2 15.4 %shard_map.236 = (bf16[1,512,1024]{2,1,0:T(8,128)(2,1)}, bf16[1,512,1024]{2,1,0:T(8,128)(2,1)}, bf16[1,512,1024]{2,1,0:T(8,128)(2,1)}) custom-call(bf16[2,3,512,1024]{3,2,1,0:T(8,128)(2,1)} %get-tuple-element.107.refs_6_.q.k.v, bf16[2,3,512,1024]{3,2,1,0:T(8,128)(2,1)} %get-tuple-element.107.refs_6_.q.k.v, ...), custom_call_target="tpu_custom_call" | custom-call | flops 10737418240 | bytes 8388608 | tf_op jit(solution)/shard_map/pallas_call | solution.py:1094
  317.1 15.5 %shard_map.238 = (bf16[1,512,1024]{2,1,0:T(8,128)(2,1)}, bf16[1,512,1024]{2,1,0:T(8,128)(2,1)}, bf16[1,512,1024]{2,1,0:T(8,128)(2,1)}) custom-call(bf16[2,3,512,1024]{3,2,1,0:T(8,128)(2,1)} %get-tuple-element.107.refs_6_.q.k.v, bf16[2,3,512,1024]{3,2,1,0:T(8,128)(2,1)} %get-tuple-element.107.refs_6_.q.k.v, ...), custom_call_target="tpu_custom_call" | custom-call | flops 10737418240 | bytes 8388608 | tf_op jit(solution)/shard_map/pallas_call | solution.py:1094
  338.5 4.9 %shard_map.240 = (bf16[1,48,512]{2,1,0:T(8,128)(2,1)}, bf16[1,16,1024]{2,1,0:T(8,128)(2,1)}, bf16[1,16,1024]{2,1,0:T(8,128)(2,1)}, bf16[1,16,1024]{2,1,0:T(8,128...) custom-call(s32[3]{0:T(128)S(1)} %add_add_fusion.meta_ref, ...), custom_call_target="tpu_custom_call" | custom-call | flops 150994944 | bytes 6635520 | tf_op jit(solution)/shard_map/pallas_call | solution.py:412
  343.4 4.9 %shard_map.241 = (bf16[1,48,512]{2,1,0:T(8,128)(2,1)}, bf16[1,16,1024]{2,1,0:T(8,128)(2,1)}, bf16[1,16,1024]{2,1,0:T(8,128)(2,1)}, bf16[1,16,1024]{2,1,0:T(8,128...) custom-call(s32[3]{0:T(128)S(1)} %add_add_fusion.1.meta_ref, ...), custom_call_target="tpu_custom_call" | custom-call | flops 150994944 | bytes 6635520 | tf_op jit(solution)/shard_map/pallas_call | solution.py:412
  359.4 2.5 collective-permute-start.44
  363.9 10.3 %shard_map.244.refs_7_ = f32[1,512,1024]{2,1,0:T(8,128)} custom-call(s32[3]{0:T(128)S(1)} %add_add_fusion.meta_ref, bf16[1,512,1024]{2,1,0:T(8,128)(2,1)} %get-tuple-element.142.refs_7_.refs_0_, bf16[1,512,1024]{2,1,0:T(8,128)(2,1)} %get-tuple-element.143.refs_1_, bf16[1,512,1024]{2,1,0:T(8,128)(2,1)} %get-tuple-element.144.refs_2_, ...), custom_call_target="tpu_custom_call" | custom-call | flops 3221225472 | bytes 16826368 | tf_op jit(solution)/shard_map/pallas_call | solution.py:412
  385.1 10.3 %shard_map.247.refs_4_ = f32[1,512,1024]{2,1,0:T(8,128)} custom-call(s32[3]{0:T(128)S(1)} %add_add_fusion.1.meta_ref, bf16[1,512,1024]{2,1,0:T(8,128)(2,1)} %get-tuple-element.150.refs_4_.refs_0_, bf16[1,512,1024]{2,1,0:T(8,128)(2,1)} %get-tuple-element.158.refs_1_, bf16[1,512,1024]{2,1,0:T(8,128)(2,1)} %get-tuple-element.159.refs_2_, ...), custom_call_target="tpu_custom_call" | custom-call | flops 3221225472 | bytes 16826368 | tf_op jit(solution)/shard_map/pallas_call | solution.py:412
  395.4 7.0 %collective-permute-done.48.refs_2_ = bf16[64,768]{1,0:T(8,128)(2,1)S(1)} collective-permute-done((bf16[64,768]{1,0:T(8,128)(2,1)S(1)}, bf16[64,768]{1,0:T(8,128)(2,1)S(1)}, u32[]{:S(2)}, u32[]{:S(2)}) %collective-permute-start.48) | collective-permute-done | bytes 98336 | tf_op jit(solution)/shard_map/ppermute | solution.py:494
  405.2 3.6 fusion
  410.8 2.7 collective-permute-start.51
  417.5 3.5 collective-permute-done.52.refs_3_
  427.5 3.2 shard_map.251
  435.9 3.2 collective-permute-done.62.refs_3_
  447.9 2.6 broadcast_select_fusion.1
  450.5 2.6 pad_maximum_fusion
  453.1 3.1 shard_map.254
  (328 shorter events, 135.9 us)
Async XLA Ops:
  6.0 24.4 %collective-permute-start.2 = (bf16[256,1536]{1,0:T(8,128)(2,1)S(1)}, bf16[256,1536]{1,0:T(8,128)(2,1)S(1)}, u32[]{:S(2)}, u32[]{:S(2)}) collective-permute-start(bf16[256,1536]{1,0:T(8,128)(2,1)S(1)} %get-tuple-element.97.refs_5_.refs_0_.refs_4_.refs_3_.refs_6_.refs_10_.refs_13_.refs_34_), channel_id=1, source_target_pairs={{0,4},{2,6},{4,0},{6,2},{8,12},{10,14},{12,8},{14,10},{16,20},{18,... | collective-permute-start | bytes 2359304 | tf_op jit(solution)/shard_map/ppermute | solution.py:494
  9.0 21.4 %collective-permute-start.1 = (bf16[256,1536]{1,0:T(8,128)(2,1)S(1)}, bf16[256,1536]{1,0:T(8,128)(2,1)S(1)}, u32[]{:S(2)}, u32[]{:S(2)}) collective-permute-start(bf16[256,1536]{1,0:T(8,128)(2,1)S(1)} %get-tuple-element.97.refs_5_.refs_0_.refs_4_.refs_3_.refs_6_.refs_10_.refs_13_.refs_34_), channel_id=1, source_target_pairs={{0,2},{2,0},{4,6},{6,4},{8,10},{10,8},{12,14},{14,12},{16,18},{18,... | collective-permute-start | bytes 2359304 | tf_op jit(solution)/shard_map/ppermute | solution.py:494
  33.8 18.2 %collective-permute-start.9 = (bf16[960,1536]{1,0:T(8,128)(2,1)S(1)}, bf16[960,1536]{1,0:T(8,128)(2,1)S(1)}, u32[]{:S(2)}, u32[]{:S(2)}) collective-permute-start(bf16[960,1536]{1,0:T(8,128)(2,1)S(1)} %shard_map.217), channel_id=1, source_target_pairs={{0,1},{1,0},{2,3},{3,2},{4,5},{5,4},{6,7},{7,6},{8,9},{9,8},{10,11... | collective-permute-start | bytes 8847368 | tf_op jit(solution)/shard_map/ppermute | solution.py:498
  33.9 17.9 %collective-permute-start.8 = (bf16[224,1536]{1,0:T(8,128)(2,1)S(1)}, bf16[224,1536]{1,0:T(8,128)(2,1)S(1)}, u32[]{:S(2)}, u32[]{:S(2)}) collective-permute-start(bf16[224,1536]{1,0:T(8,128)(2,1)S(1)} %get-tuple-element.100), channel_id=1, source_target_pairs={{0,4},{2,6},{4,0},{6,2},{8,12},{10,14},{12,8},{14,10},{16,20},{18,... | collective-permute-start | bytes 2064392 | tf_op jit(solution)/shard_map/ppermute | solution.py:494
  56.0 20.7 %collective-permute-start.12 = (bf16[160,1536]{1,0:T(8,128)(2,1)S(1)}, bf16[160,1536]{1,0:T(8,128)(2,1)S(1)}, u32[]{:S(2)}, u32[]{:S(2)}) collective-permute-start(bf16[160,1536]{1,0:T(8,128)(2,1)S(1)} %get-tuple-element.103), channel_id=1, source_target_pairs={{0,4},{2,6},{4,0},{6,2},{8,12},{10,14},{12,8},{14,10},{16,20},{18,... | collective-permute-start | bytes 1474568 | tf_op jit(solution)/shard_map/ppermute | solution.py:494
  57.5 19.1 %collective-permute-start.11 = (bf16[160,1536]{1,0:T(8,128)(2,1)S(1)}, bf16[160,1536]{1,0:T(8,128)(2,1)S(1)}, u32[]{:S(2)}, u32[]{:S(2)}) collective-permute-start(bf16[160,1536]{1,0:T(8,128)(2,1)S(1)} %copy-done.46), channel_id=1, source_target_pairs={{0,2},{2,0},{4,6},{6,4},{8,10},{10,8},{12,14},{14,12},{16,18},{18,... | collective-permute-start | bytes 1474568 | tf_op jit(solution)/shard_map/ppermute | solution.py:494
  76.9 24.8 %collective-permute-start.18 = (bf16[224,1536]{1,0:T(8,128)(2,1)S(1)}, bf16[224,1536]{1,0:T(8,128)(2,1)S(1)}, u32[]{:S(2)}, u32[]{:S(2)}) collective-permute-start(bf16[224,1536]{1,0:T(8,128)(2,1)S(1)} %get-tuple-element.108), channel_id=1, source_target_pairs={{0,4},{2,6},{4,0},{6,2},{8,12},{10,14},{12,8},{14,10},{16,20},{18,... | collective-permute-start | bytes 2064392 | tf_op jit(solution)/shard_map/ppermute | solution.py:494
  78.2 23.4 %collective-permute-start.17 = (bf16[224,1536]{1,0:T(8,128)(2,1)S(1)}, bf16[224,1536]{1,0:T(8,128)(2,1)S(1)}, u32[]{:S(2)}, u32[]{:S(2)}) collective-permute-start(bf16[224,1536]{1,0:T(8,128)(2,1)S(1)} %copy-done.44), channel_id=1, source_target_pairs={{0,2},{2,0},{4,6},{6,4},{8,10},{10,8},{12,14},{14,12},{16,18},{18,... | collective-permute-start | bytes 2064392 | tf_op jit(solution)/shard_map/ppermute | solution.py:494
  79.7 21.9 %collective-permute-start.20 = (bf16[64,1536]{1,0:T(8,128)(2,1)S(1)}, bf16[64,1536]{1,0:T(8,128)(2,1)S(1)}, u32[]{:S(2)}, u32[]{:S(2)}) collective-permute-start(bf16[64,1536]{1,0:T(8,128)(2,1)S(1)} %get-tuple-element.110), channel_id=1, source_target_pairs={{0,16},{2,18},{4,20},{6,22},{8,24},{10,26},{12,28},{14,30},{16,0},... | collective-permute-start | bytes 589832 | tf_op jit(solution)/shard_map/ppermute | solution.py:494
  80.9 20.7 %collective-permute-start.19 = (bf16[128,1536]{1,0:T(8,128)(2,1)S(1)}, bf16[128,1536]{1,0:T(8,128)(2,1)S(1)}, u32[]{:S(2)}, u32[]{:S(2)}) collective-permute-start(bf16[128,1536]{1,0:T(8,128)(2,1)S(1)} %get-tuple-element.109), channel_id=1, source_target_pairs={{0,8},{2,10},{4,12},{6,14},{8,0},{10,2},{12,4},{14,6},{16,24},{18,... | collective-permute-start | bytes 1179656 | tf_op jit(solution)/shard_map/ppermute | solution.py:494
  104.8 24.1 %collective-permute-start.23 = (bf16[832,1536]{1,0:T(8,128)(2,1)S(1)}, bf16[832,1536]{1,0:T(8,128)(2,1)S(1)}, u32[]{:S(2)}, u32[]{:S(2)}) collective-permute-start(bf16[832,1536]{1,0:T(8,128)(2,1)S(1)} %shard_map.224.refs_0_), channel_id=1, source_target_pairs={{0,1},{1,0},{2,3},{3,2},{4,5},{5,4},{6,7},{7,6},{8,9},{9,8},{10,11... | collective-permute-start | bytes 7667720 | tf_op jit(solution)/shard_map/ppermute | solution.py:498
  104.9 24.0 %collective-permute-start.22 = (bf16[288,1536]{1,0:T(8,128)(2,1)S(1)}, bf16[288,1536]{1,0:T(8,128)(2,1)S(1)}, u32[]{:S(2)}, u32[]{:S(2)}) collective-permute-start(bf16[288,1536]{1,0:T(8,128)(2,1)S(1)} %get-tuple-element.115), channel_id=1, source_target_pairs={{0,4},{2,6},{4,0},{6,2},{8,12},{10,14},{12,8},{14,10},{16,20},{18,... | collective-permute-start | bytes 2654216 | tf_op jit(solution)/shard_map/ppermute | solution.py:494
  105.9 23.0 %collective-permute-start.21 = (bf16[288,1536]{1,0:T(8,128)(2,1)S(1)}, bf16[288,1536]{1,0:T(8,128)(2,1)S(1)}, u32[]{:S(2)}, u32[]{:S(2)}) collective-permute-start(bf16[288,1536]{1,0:T(8,128)(2,1)S(1)} %copy-done.38), channel_id=1, source_target_pairs={{0,2},{2,0},{4,6},{6,4},{8,10},{10,8},{12,14},{14,12},{16,18},{18,... | collective-permute-start | bytes 2654216 | tf_op jit(solution)/shard_map/ppermute | solution.py:494
  106.4 22.4 %collective-permute-start.25 = (bf16[64,1536]{1,0:T(8,128)(2,1)S(1)}, bf16[64,1536]{1,0:T(8,128)(2,1)S(1)}, u32[]{:S(2)}, u32[]{:S(2)}) collective-permute-start(bf16[64,1536]{1,0:T(8,128)(2,1)S(1)} %get-tuple-element.117.refs_4_), channel_id=1, source_target_pairs={{0,16},{2,18},{4,20},{6,22},{8,24},{10,26},{12,28},{14,30},{16,0},... | collective-permute-start | bytes 589832 | tf_op jit(solution)/shard_map/ppermute | solution.py:494
  107.6 21.2 %collective-permute-start.24 = (bf16[128,1536]{1,0:T(8,128)(2,1)S(1)}, bf16[128,1536]{1,0:T(8,128)(2,1)S(1)}, u32[]{:S(2)}, u32[]{:S(2)}) collective-permute-start(bf16[128,1536]{1,0:T(8,128)(2,1)S(1)} %get-tuple-element.116), channel_id=1, source_target_pairs={{0,8},{2,10},{4,12},{6,14},{8,0},{10,2},{12,4},{14,6},{16,24},{18,... | collective-permute-start | bytes 1179656 | tf_op jit(solution)/shard_map/ppermute | solution.py:494
  133.0 22.1 %collective-permute-start.28 = (bf16[288,1536]{1,0:T(8,128)(2,1)S(1)}, bf16[288,1536]{1,0:T(8,128)(2,1)S(1)}, u32[]{:S(2)}, u32[]{:S(2)}) collective-permute-start(bf16[288,1536]{1,0:T(8,128)(2,1)S(1)} %get-tuple-element.122), channel_id=1, source_target_pairs={{0,4},{2,6},{4,0},{6,2},{8,12},{10,14},{12,8},{14,10},{16,20},{18,... | collective-permute-start | bytes 2654216 | tf_op jit(solution)/shard_map/ppermute | solution.py:494
  134.1 21.7 %collective-permute-start.27 = (bf16[288,1536]{1,0:T(8,128)(2,1)S(1)}, bf16[288,1536]{1,0:T(8,128)(2,1)S(1)}, u32[]{:S(2)}, u32[]{:S(2)}) collective-permute-start(bf16[288,1536]{1,0:T(8,128)(2,1)S(1)} %copy-done.36), channel_id=1, source_target_pairs={{0,2},{2,0},{4,6},{6,4},{8,10},{10,8},{12,14},{14,12},{16,18},{18,... | collective-permute-start | bytes 2654216 | tf_op jit(solution)/shard_map/ppermute | solution.py:494
  157.5 24.5 %collective-permute-start.30 = (bf16[704,1536]{1,0:T(8,128)(2,1)}, bf16[704,1536]{1,0:T(8,128)(2,1)S(1)}, u32[]{:S(2)}, u32[]{:S(2)}) collective-permute-start(bf16[704,1536]{1,0:T(8,128)(2,1)} %shard_map.230.refs_20_), channel_id=1, source_target_pairs={{0,1},{1,0},{2,3},{3,2},{4,5},{5,4},{6,7},{7,6},{8,9},{9,8},{10,11... | collective-permute-start | bytes 6488072 | tf_op jit(solution)/shard_map/ppermute | solution.py:498
  313.6 19.0 %collective-permute-start.36 = (bf16[64,1536]{1,0:T(8,128)(2,1)S(1)}, bf16[64,1536]{1,0:T(8,128)(2,1)S(1)}, u32[]{:S(2)}, u32[]{:S(2)}) collective-permute-start(bf16[64,1536]{1,0:T(8,128)(2,1)S(1)} %get-tuple-element.147), channel_id=1, source_target_pairs={{0,2},{2,0},{4,6},{6,4},{8,10},{10,8},{12,14},{14,12},{16,18},{18,... | collective-permute-start | bytes 589832 | tf_op jit(solution)/shard_map/ppermute | solution.py:494
  314.2 18.4 %collective-permute-start.37 = (bf16[64,1536]{1,0:T(8,128)(2,1)S(1)}, bf16[64,1536]{1,0:T(8,128)(2,1)S(1)}, u32[]{:S(2)}, u32[]{:S(2)}) collective-permute-start(bf16[64,1536]{1,0:T(8,128)(2,1)S(1)} %get-tuple-element.148), channel_id=1, source_target_pairs={{0,4},{2,6},{4,0},{6,2},{8,12},{10,14},{12,8},{14,10},{16,20},{18,... | collective-permute-start | bytes 589832 | tf_op jit(solution)/shard_map/ppermute | solution.py:494
  334.1 24.1 %collective-permute-start.39 = (bf16[32,1536]{1,0:T(8,128)(2,1)S(1)}, bf16[32,1536]{1,0:T(8,128)(2,1)S(1)}, u32[]{:S(2)}, u32[]{:S(2)}) collective-permute-start(bf16[32,1536]{1,0:T(8,128)(2,1)S(1)} %get-tuple-element.154), channel_id=1, source_target_pairs={{0,8},{2,10},{4,12},{6,14},{8,0},{10,2},{12,4},{14,6},{16,24},{18,... | collective-permute-start | bytes 294920 | tf_op jit(solution)/shard_map/ppermute | solution.py:494
  335.4 22.8 %collective-permute-start.40 = (bf16[32,1536]{1,0:T(8,128)(2,1)S(1)}, bf16[32,1536]{1,0:T(8,128)(2,1)S(1)}, u32[]{:S(2)}, u32[]{:S(2)}) collective-permute-start(bf16[32,1536]{1,0:T(8,128)(2,1)S(1)} %get-tuple-element.155), channel_id=1, source_target_pairs={{0,16},{2,18},{4,20},{6,22},{8,24},{10,26},{12,28},{14,30},{16,0},... | collective-permute-start | bytes 294920 | tf_op jit(solution)/shard_map/ppermute | solution.py:494
  337.1 21.1 %collective-permute-start.41 = (bf16[32,1536]{1,0:T(8,128)(2,1)S(1)}, bf16[32,1536]{1,0:T(8,128)(2,1)S(1)}, u32[]{:S(2)}, u32[]{:S(2)}) collective-permute-start(bf16[32,1536]{1,0:T(8,128)(2,1)S(1)} %get-tuple-element.156), channel_id=1, source_target_pairs={{0,24},{2,26},{4,28},{6,30},{8,16},{10,18},{12,20},{14,22},{16,8},... | collective-permute-start | bytes 294920 | tf_op jit(solution)/shard_map/ppermute | solution.py:494
  359.4 17.9 %collective-permute-start.44 = (bf16[32,1536]{1,0:T(8,128)(2,1)S(1)}, bf16[32,1536]{1,0:T(8,128)(2,1)S(1)}, u32[]{:S(2)}, u32[]{:S(2)}) collective-permute-start(bf16[32,1536]{1,0:T(8,128)(2,1)S(1)} %shard_map.243.refs_19_.refs_0_), channel_id=1, source_target_pairs={{0,24},{2,26},{4,28},{6,30},{8,16},{10,18},{12,20},{14,22},{16,8},... | collective-permute-start | bytes 294920 | tf_op jit(solution)/shard_map/ppermute | solution.py:494
  378.6 25.1 %collective-permute-start.55 = (bf16[128,1536]{1,0:T(8,128)(2,1)S(1)}, bf16[128,1536]{1,0:T(8,128)(2,1)S(1)}, u32[]{:S(2)}, u32[]{:S(2)}) collective-permute-start(bf16[128,1536]{1,0:T(8,128)(2,1)S(1)} %shard_map.246.refs_19_.refs_0_), channel_id=1, source_target_pairs={{0,6},{2,4},{4,2},{6,0},{8,14},{10,12},{12,10},{14,8},{16,22},{18,... | collective-permute-start | bytes 1179656 | tf_op jit(solution)/shard_map/ppermute | solution.py:494
  380.5 23.2 %collective-permute-start.54 = (bf16[128,1536]{1,0:T(8,128)(2,1)S(1)}, bf16[128,1536]{1,0:T(8,128)(2,1)S(1)}, u32[]{:S(2)}, u32[]{:S(2)}) collective-permute-start(bf16[128,1536]{1,0:T(8,128)(2,1)S(1)} %shard_map.246.refs_19_.refs_0_), channel_id=1, source_target_pairs={{0,4},{2,6},{4,0},{6,2},{8,12},{10,14},{12,8},{14,10},{16,20},{18,... | collective-permute-start | bytes 1179656 | tf_op jit(solution)/shard_map/ppermute | solution.py:494
  381.6 22.1 %collective-permute-start.53 = (bf16[128,1536]{1,0:T(8,128)(2,1)S(1)}, bf16[128,1536]{1,0:T(8,128)(2,1)S(1)}, u32[]{:S(2)}, u32[]{:S(2)}) collective-permute-start(bf16[128,1536]{1,0:T(8,128)(2,1)S(1)} %shard_map.246.refs_19_.refs_0_), channel_id=1, source_target_pairs={{0,2},{2,0},{4,6},{6,4},{8,10},{10,8},{12,14},{14,12},{16,18},{18,... | collective-permute-start | bytes 1179656 | tf_op jit(solution)/shard_map/ppermute | solution.py:494
  382.2 20.2 %collective-permute-start.48 = (bf16[64,768]{1,0:T(8,128)(2,1)S(1)}, bf16[64,768]{1,0:T(8,128)(2,1)S(1)}, u32[]{:S(2)}, u32[]{:S(2)}) collective-permute-start(bf16[64,768]{1,0:T(8,128)(2,1)S(1)} %get-tuple-element.174), channel_id=1, source_target_pairs={{0,4},{2,6},{4,0},{6,2},{8,12},{10,14},{12,8},{14,10},{16,20},{18,... | collective-permute-start | bytes 294920 | tf_op jit(solution)/shard_map/ppermute | solution.py:494
  383.1 19.3 %collective-permute-start.49 = (bf16[64,768]{1,0:T(8,128)(2,1)S(1)}, bf16[64,768]{1,0:T(8,128)(2,1)S(1)}, u32[]{:S(2)}, u32[]{:S(2)}) collective-permute-start(bf16[64,768]{1,0:T(8,128)(2,1)S(1)} %get-tuple-element.175), channel_id=1, source_target_pairs={{0,6},{2,4},{4,2},{6,0},{8,14},{10,12},{12,10},{14,8},{16,22},{18,... | collective-permute-start | bytes 294920 | tf_op jit(solution)/shard_map/ppermute | solution.py:494
  405.1 19.1 %collective-permute-start.59 = (bf16[512,1536]{1,0:T(8,128)(2,1)S(1)}, bf16[512,1536]{1,0:T(8,128)(2,1)S(1)}, u32[]{:S(2)}, u32[]{:S(2)}) collective-permute-start(bf16[512,1536]{1,0:T(8,128)(2,1)S(1)} %shard_map.249.refs_4_.refs_0_.refs_2_), channel_id=1, source_target_pairs={{0,1},{1,0},{2,3},{3,2},{4,5},{5,4},{6,7},{7,6},{8,9},{9,8},{10,11... | collective-permute-start | bytes 4718600 | tf_op jit(solution)/shard_map/ppermute | solution.py:498
  408.8 37.6 %collective-permute-start.46 = (f32[2,256,1024]{2,1,0:T(8,128)}, f32[2,256,1024]{2,1,0:T(8,128)}, u32[]{:S(2)}, u32[]{:S(2)}) collective-permute-start(f32[2,256,1024]{2,1,0:T(8,128)} %fusion), channel_id=1, source_target_pairs={{0,1},{1,0},{2,3},{3,2},{4,5},{5,4},{6,7},{7,6},{8,9},{9,8},{10,11... | collective-permute-start | bytes 6291464 | tf_op jit(solution)/shard_map/ppermute | solution.py:498
  410.0 32.8 %collective-permute-start.31 = (bf16[2,256,1024]{2,1,0:T(8,128)(2,1)}, bf16[2,256,1024]{2,1,0:T(8,128)(2,1)}, u32[]{:S(2)}, u32[]{:S(2)}) collective-permute-start(bf16[2,256,1024]{2,1,0:T(8,128)(2,1)} %constant_dynamic-slice_fusion), channel_id=1, source_target_pairs={{0,1},{1,0},{2,3},{3,2},{4,5},{5,4},{6,7},{7,6},{8,9},{9,8},{10,11... | collective-permute-start | bytes 3145736 | tf_op jit(solution)/shard_map/ppermute | solution.py:498
  (113 other events, 734.3 us)
